TPU v7x, 32 devices: a whole 2x2x4 slice. The times are simulated.
32 devices in a mesh: az: 8 (over z, y), rg: 4 (over x, core).
Axes of the slice: x: 2, y: 2, z: 4, core: 2. Of those that a mesh axis runs over, the one named last changes fastest.
Arguments:
- echoes: bfloat16 [2, 8192, 16384], P(None, 'rg', 'az'), may hold values from -6 to 6
- replica: bfloat16 [2, 2048], replicated, may hold values from -0.125 to 0.125
- shifts: int32 [512, 8], replicated, may hold values from 0 to 16, as said below
- tap_counts: int32 [512], replicated, may hold values from 1 to 8
- interp_weights: float32 [512, 8], replicated, may hold values from -2 to 2
- fm_rates: float32 [512], replicated, may hold values from 50 to 1000
Outputs:
- focused_image: float32 [2, 8192, 16384], P(None, ('rg', 'az'))
Inputs may be any that keep to these rules, and one draw needn't show every extreme that they name: `shifts`: in some range band and Doppler block the shift is 16 while that band uses all 8 taps.
All inputs are finite; a program needn't handle non-finite values.
Results may differ from a plain program's by a relative error of at most 0.0029.
Values may be sent and summed in bfloat16 or wider, within the bound.
A program may use at most 320 MiB of HBM per device.

v0:
```python
import functools
import math

import jax
import jax.numpy as jnp
import numpy as np
from jax import lax
from jax.experimental import pallas as pl
from jax.experimental.pallas import tpu as pltpu
from jax.sharding import PartitionSpec as P

SIDE = 128
INTERP_TAPS = 8
MAX_SHIFT = 16
BAND_BINS = 16
DOPPLER_BLOCKS = 8
CHUNKS = 2
RIM_ROWS = 32
VMEM = 56 * 1024 * 1024


def transform_tables():
    k = np.arange(SIDE)
    angle = 2.0 * np.pi * ((k[:, None] * k[None, :]) % SIDE) / SIDE
    c, s = np.cos(angle), np.sin(angle)
    forward = np.block([[c, s], [-s, c]])
    inverse = np.block([[c, -s], [s, c]])
    twist = 2.0 * np.pi * (k[:, None] * k[None, :]) / (SIDE * SIDE)
    return forward, inverse, np.cos(twist), np.sin(twist)


def split_const(matrix):
    high = jnp.asarray(matrix, jnp.float32).astype(jnp.bfloat16)
    low_np = np.asarray(matrix, np.float64) - np.asarray(
        np.asarray(matrix, np.float32).astype(jnp.bfloat16), np.float64
    )
    return jnp.stack([high, jnp.asarray(low_np, jnp.float32).astype(jnp.bfloat16)])


def split_data(value):
    high = value.astype(jnp.bfloat16)
    return high, (value - high.astype(jnp.float32)).astype(jnp.bfloat16)


NN = (((1,), (0,)), ((), ()))
NT = (((1,), (1,)), ((), ()))


def mm(a, b, dims):
    return lax.dot_general(a, b, dims, preferred_element_type=jnp.float32)


def mm2(table, data, dims):
    return mm(table[0], data, dims) + mm(table[1], data, dims)


def mm3(table, value, dims):
    high, low = split_data(value)
    return mm(table[0], high, dims) + (mm(table[1], high, dims) + mm(table[0], low, dims))


def compress_kernel(chunk, block_rows, local_rows, w_ref, own_ref, rim_ref, out_ref, window):
    dest = pl.program_id(1)
    own_rows = own_ref.shape[1]

    @pl.when(dest == 0)
    def _():
        window[:, :own_rows, :] = own_ref[...]
        window[:, own_rows:, :] = rim_ref[...]

    start = pl.multiple_of(dest * local_rows + chunk * block_rows, block_rows)
    span = w_ref.shape[2]
    total = mm(w_ref[0], window[0, pl.ds(start, span), :], NN)
    total = total + mm(w_ref[1], window[1, pl.ds(start, span), :], NN)
    total = total.astype(jnp.bfloat16)
    out_ref[0, 0] = total[:block_rows]
    out_ref[0, 1] = total[block_rows:]


def compress(weights, echoes, rim, chunk, az_count, local_rows):
    range_dev, lines = echoes.shape[1], echoes.shape[2]
    taps = rim.shape[1]
    block_rows = local_rows // CHUNKS
    tile = math.gcd(512, lines)
    span = weights.shape[2]
    return pl.pallas_call(
        functools.partial(compress_kernel, chunk, block_rows, local_rows),
        out_shape=jax.ShapeDtypeStruct((az_count, 2, block_rows, lines), jnp.bfloat16),
        grid=(lines // tile, az_count),
        in_specs=[
            pl.BlockSpec(weights.shape, lambda l, j: (0, 0, 0)),
            pl.BlockSpec((2, range_dev, tile), lambda l, j: (0, 0, l)),
            pl.BlockSpec((2, taps, tile), lambda l, j: (0, 0, l)),
        ],
        out_specs=pl.BlockSpec((1, 2, block_rows, tile), lambda l, j: (j, 0, 0, l)),
        scratch_shapes=[pltpu.VMEM((2, range_dev + taps, tile), jnp.bfloat16)],
        compiler_params=pltpu.CompilerParams(vmem_limit_bytes=VMEM),
        cost_estimate=pl.CostEstimate(
            flops=8 * az_count * block_rows * span * lines,
            bytes_accessed=4 * lines * (2 * range_dev + taps),
            transcendentals=0,
        ),
        name=f"compress_{chunk}",
    )(weights, echoes, rim)


def compress_weights(replica, block_rows):
    taps = replica.shape[1]
    span = taps + block_rows

    def banded(vector):
        cycled = jnp.concatenate([vector, jnp.zeros((span + 1 - taps,), vector.dtype)])
        return jnp.tile(cycled, block_rows)[: block_rows * span].reshape(block_rows, span)

    real_rows = banded(replica[0])
    imag_rows = banded(replica[1])
    return jnp.stack(
        [
            jnp.concatenate([real_rows, -imag_rows], axis=0),
            jnp.concatenate([imag_rows, real_rows], axis=0),
        ]
    )


def forward_kernel(table_ref, cos_ref, sin_ref, in_ref, *rest):
    out_ref, data = rest[-2], rest[-1]
    az_count, _, rows, lines = in_ref.shape
    per = lines // SIDE
    for source in range(az_count):
        for c in range(2):
            piece = in_ref[source, c].astype(jnp.float32)
            data[:, c * SIDE + source * per : c * SIDE + (source + 1) * per, :] = piece.reshape(
                rows, per, SIDE
            )

    def pair(i, _):
        both = jnp.concatenate([data[2 * i], data[2 * i + 1]], axis=1).astype(jnp.bfloat16)
        first = mm2(table_ref, both, NN)
        cosine, sine = cos_ref[...], sin_ref[...]
        turned = []
        for k in range(2):
            real = first[:SIDE, k * SIDE : (k + 1) * SIDE]
            imag = first[SIDE:, k * SIDE : (k + 1) * SIDE]
            turned.append(
                jnp.concatenate(
                    [real * cosine + imag * sine, imag * cosine - real * sine], axis=1
                )
            )
        second = mm3(table_ref, jnp.concatenate(turned, axis=0), NT)
        for k in range(2):
            out_ref[0, 2 * i + k] = second[:SIDE, k * SIDE : (k + 1) * SIDE]
            out_ref[1, 2 * i + k] = second[SIDE:, k * SIDE : (k + 1) * SIDE]
        return 0

    lax.fori_loop(0, rows // 2, pair, 0, unroll=2)


def forward(tables, lines_in, held, first_block, total_rows):
    table, cosine, sine = tables
    az_count, _, rows, lines = lines_in.shape
    whole2 = lambda i: (0, 0)
    in_specs = [
        pl.BlockSpec(table.shape, lambda i: (0, 0, 0)),
        pl.BlockSpec((SIDE, SIDE), whole2),
        pl.BlockSpec((SIDE, SIDE), whole2),
        pl.BlockSpec((az_count, 2, BAND_BINS, lines), lambda i: (0, 0, i, 0)),
    ]
    operands = [table, cosine, sine, lines_in]
    aliases = {}
    if held is not None:
        in_specs.append(pl.BlockSpec(memory_space=pl.ANY))
        operands.append(held)
        aliases = {4: 0}
    return pl.pallas_call(
        forward_kernel,
        out_shape=jax.ShapeDtypeStruct((2, total_rows, SIDE, SIDE), jnp.float32),
        grid=(rows // BAND_BINS,),
        in_specs=in_specs,
        out_specs=pl.BlockSpec((2, BAND_BINS, SIDE, SIDE), lambda i: (0, first_block + i, 0, 0)),
        scratch_shapes=[pltpu.VMEM((BAND_BINS, 2 * SIDE, SIDE), jnp.float32)],
        input_output_aliases=aliases,
        compiler_params=pltpu.CompilerParams(vmem_limit_bytes=VMEM),
        cost_estimate=pl.CostEstimate(
            flops=rows * 5 * 2 * 2 * SIDE * 2 * SIDE * SIDE * 2,
            bytes_accessed=rows * SIDE * SIDE * 12,
            transcendentals=0,
        ),
        name=f"forward_at_{first_block}",
    )(*operands)


def focus_kernel(
    shift_ref, weight_ref, table_ref, cos_ref, sin_ref, pcos_ref, psin_ref,
    spec0, spec1, spec2, out_ref, window, moved, image
):
    band = pl.program_id(0)
    for k, ref in enumerate((spec0, spec1, spec2)):
        keep = BAND_BINS if k < 2 else INTERP_TAPS
        window[:, k * BAND_BINS : k * BAND_BINS + keep] = ref[:, :keep]
    deep = SIDE // DOPPLER_BLOCKS
    taps = [weight_ref[band, t] for t in range(INTERP_TAPS)]

    def block(d, _):
        shift = shift_ref[band, d]
        spot = pl.ds(pl.multiple_of(d * deep, deep), deep)
        pcos, psin = pcos_ref[0, spot, :], psin_ref[0, spot, :]
        sums = []
        for half in range(2):
            rows = BAND_BINS // 2
            parts = []
            for c in range(2):
                total = taps[0] * window[c, pl.ds(shift + half * rows, rows), spot, :]
                for t in range(1, INTERP_TAPS):
                    total = total + taps[t] * window[c, pl.ds(shift + half * rows + t, rows), spot, :]
                parts.append(total)
            real, imag = parts
            put = slice(half * rows, (half + 1) * rows)
            moved[put, spot, :] = real * pcos + imag * psin
            low = pl.ds(pl.multiple_of(SIDE + d * deep, deep), deep)
            moved[put, low, :] = imag * pcos - real * psin
        return 0

    lax.fori_loop(0, DOPPLER_BLOCKS, block, 0)

    def pair(i, _):
        both = jnp.concatenate([moved[2 * i], moved[2 * i + 1]], axis=1)
        first = mm3(table_ref, both, NN)
        cosine, sine = cos_ref[...], sin_ref[...]
        turned = []
        for k in range(2):
            real = first[:SIDE, k * SIDE : (k + 1) * SIDE]
            imag = first[SIDE:, k * SIDE : (k + 1) * SIDE]
            turned.append(
                jnp.concatenate(
                    [real * cosine - imag * sine, imag * cosine + real * sine], axis=1
                )
            )
        second = mm2(table_ref, jnp.concatenate(turned, axis=0).astype(jnp.bfloat16), NT)
        second = second * (1.0 / (SIDE * SIDE))
        for k in range(2):
            image[2 * i + k] = second[:, k * SIDE : (k + 1) * SIDE]
        return 0

    lax.fori_loop(0, BAND_BINS // 2, pair, 0, unroll=2)
    group = 16
    for c in range(2):
        for g in range(SIDE // group):
            piece = image[:, c * SIDE + g * group : c * SIDE + (g + 1) * group, :]
            out_ref[c, :, g * group * SIDE : (g + 1) * group * SIDE] = piece.reshape(
                BAND_BINS, group * SIDE
            )


def focus(shifts, weights, tables, pcos, psin, spectrum, local_rows):
    table, cosine, sine = tables
    whole2 = lambda i, *_: (0, 0)

    def part(k):
        return pl.BlockSpec((2, BAND_BINS, SIDE, SIDE), lambda i, *_: (0, i + k, 0, 0))

    phase_spec = pl.BlockSpec((1, SIDE, SIDE), lambda i, *_: (i, 0, 0))
    return pl.pallas_call(
        focus_kernel,
        out_shape=jax.ShapeDtypeStruct((2, local_rows, SIDE * SIDE), jnp.float32),
        grid_spec=pltpu.PrefetchScalarGridSpec(
            num_scalar_prefetch=2,
            grid=(local_rows // BAND_BINS,),
            in_specs=[
                pl.BlockSpec(table.shape, lambda i, *_: (0, 0, 0)),
                pl.BlockSpec((SIDE, SIDE), whole2),
                pl.BlockSpec((SIDE, SIDE), whole2),
                phase_spec,
                phase_spec,
                part(0),
                part(1),
                part(2),
            ],
            out_specs=pl.BlockSpec((2, BAND_BINS, SIDE * SIDE), lambda i, *_: (0, i, 0)),
            scratch_shapes=[
                pltpu.VMEM((2, 2 * BAND_BINS + INTERP_TAPS, SIDE, SIDE), jnp.float32),
                pltpu.VMEM((BAND_BINS, 2 * SIDE, SIDE), jnp.float32),
                pltpu.VMEM((BAND_BINS, 2 * SIDE, SIDE), jnp.float32),
            ],
        ),
        compiler_params=pltpu.CompilerParams(vmem_limit_bytes=VMEM),
        name="focus",
    )(shifts, weights, table, cosine, sine, pcos, psin, spectrum, spectrum, spectrum)


def per_device(echoes, replica, shifts, tap_counts, interp_weights, fm_rates):
    tap_total = replica.shape[1]
    range_dev = echoes.shape[1]
    az_count = lax.axis_size("az")
    rg_count = lax.axis_size("rg")
    local_rows = range_dev // az_count
    block_rows = local_rows // CHUNKS
    bands_here = local_rows // BAND_BINS
    az_pos = lax.axis_index("az")
    rg_pos = lax.axis_index("rg")

    rim = lax.ppermute(
        echoes[:, :tap_total], "rg", [(i, i - 1) for i in range(1, rg_count)]
    )
    weights = compress_weights(replica, block_rows)
    forward_m, inverse_m, twist_cos, twist_sin = transform_tables()
    cosine = jnp.asarray(twist_cos, jnp.float32)
    sine = jnp.asarray(twist_sin, jnp.float32)
    forward_tables = (split_const(forward_m), cosine, sine)
    inverse_tables = (split_const(inverse_m), cosine, sine)

    band_first = (rg_pos * range_dev + az_pos * local_rows) // BAND_BINS
    band_shift = lax.dynamic_slice_in_dim(shifts, band_first, bands_here)
    band_taps = lax.dynamic_slice_in_dim(tap_counts, band_first, bands_here)
    band_weight = lax.dynamic_slice_in_dim(interp_weights, band_first, bands_here)
    tap_index = lax.broadcasted_iota(jnp.int32, (bands_here, INTERP_TAPS), 1)
    live_weight = jnp.where(tap_index < band_taps[:, None], band_weight, 0.0)
    band_rate = lax.dynamic_slice_in_dim(fm_rates, band_first, bands_here)
    total_lines = SIDE * SIDE
    doppler = SIDE * lax.broadcasted_iota(jnp.int32, (SIDE, SIDE), 0) + lax.broadcasted_iota(
        jnp.int32, (SIDE, SIDE), 1
    )
    signed = (
        jnp.where(doppler < total_lines // 2, doppler, doppler - total_lines).astype(jnp.float32)
        / total_lines
    )
    phases = math.pi * band_rate[:, None, None] * (signed * signed)[None]
    pcos = jnp.cos(phases)
    psin = jnp.sin(phases)

    def turn(chunk):
        part = compress(weights, echoes, rim, chunk, az_count, local_rows)
        return lax.all_to_all(part, "az", split_axis=0, concat_axis=0, tiled=True)

    turned = [turn(chunk) for chunk in range(CHUNKS)]
    place = [a * rg_count + g for g in range(rg_count) for a in range(az_count)]
    beyond = lax.ppermute(
        turned[0][:, :, :RIM_ROWS], ("az", "rg"), list(zip(place[1:], place[:-1]))
    )
    total_rows = local_rows + RIM_ROWS
    step = block_rows // BAND_BINS
    spectrum = forward(forward_tables, turned[0], None, 0, total_rows)
    spectrum = forward(forward_tables, beyond, spectrum, CHUNKS * step, total_rows)
    for chunk in range(1, CHUNKS):
        spectrum = forward(forward_tables, turned[chunk], spectrum, chunk * step, total_rows)
    return focus(band_shift, live_weight, inverse_tables, pcos, psin, spectrum, local_rows)


def solution(mesh):
    return jax.shard_map(
        per_device,
        mesh=mesh,
        in_specs=(P(None, "rg", "az"), P(), P(), P(), P(), P()),
        out_specs=P(None, ("rg", "az"), None),
        check_vma=False,
    )
```

profile of v0, /device:TPU:29, one launch (start us, length us, event | category | flops | bytes accessed | tf_op | source)
XLA Modules:
  0.0 694.5 jit_solution(15374065884512527461)
XLA Ops:
  0.0 2.7 collective-permute-start
  2.7 0.8 slice_reduce_fusion
  3.6 0.7 tile.9
  5.1 0.7 tile.21
  6.7 1.6 pad_maximum_fusion.w_ref
  8.3 176.8 %collective-permute-done.rim_ref = bf16[2,2048,2048]{2,1,0:T(8,128)(2,1)} collective-permute-done((bf16[2,2048,2048]{2,1,0:T(8,128)(2,1)}, bf16[2,2048,2048]{2,1,0:T(8,128)(2,1)}, u32[]{:S(2)}, u32[]{:S(2)}) %collective-permute-start) | collective-permute-done | bytes 16777248 | tf_op jit(solution)/shard_map/ppermute | solution.py:301
  185.2 59.0 %compress_0.1 = bf16[8,2,128,2048]{3,2,1,0:T(8,128)(2,1)} custom-call(bf16[2,256,2176]{2,1,0:T(8,128)(2,1)} %pad_maximum_fusion.w_ref, bf16[2,2048,2048]{2,1,0:T(8,128)(2,1)} %own_ref.3, bf16[2,2048,2048]{2,1,0:T(8,128)(2,1)} %collective-permute-done.rim_ref), custom_call_target="tpu_custom_call" | custom-call | flops 36507222016 | bytes 50331648 | tf_op jit(solution)/shard_map/compress_0/pallas_call | solution.py:86
  244.2 5.4 all-to-all-start.1
  249.6 59.0 %compress_1.1 = bf16[8,2,128,2048]{3,2,1,0:T(8,128)(2,1)} custom-call(bf16[2,256,2176]{2,1,0:T(8,128)(2,1)} %pad_maximum_fusion.w_ref, bf16[2,2048,2048]{2,1,0:T(8,128)(2,1)} %own_ref.3, bf16[2,2048,2048]{2,1,0:T(8,128)(2,1)} %collective-permute-done.rim_ref), custom_call_target="tpu_custom_call" | custom-call | flops 36507222016 | bytes 50331648 | tf_op jit(solution)/shard_map/compress_1/pallas_call | solution.py:86
  308.6 66.2 %all-to-all-done.1.in_ref = bf16[8,2,128,2048]{3,2,1,0:T(8,128)(2,1)} async-done(((bf16[8,2,128,2048]{3,2,1,0:T(8,128)(2,1)}), bf16[8,2,128,2048]{3,2,1,0:T(8,128)(2,1)}, u32[]{:S(2)}, u32[]{:S(2)}) %all-to-all-start.1) | async-done | bytes 8388640 | tf_op jit(solution)/shard_map/all_to_all | solution.py:332
  374.8 29.9 %all-to-all-start = ((bf16[8,2,128,2048]{3,2,1,0:T(8,128)(2,1)}), bf16[8,2,128,2048]{3,2,1,0:T(8,128)(2,1)}, u32[]{:S(2)}, u32[]{:S(2)}) async-start(bf16[8,2,128,2048]{3,2,1,0:T(8,128)(2,1)} %compress_1.1), calls=%async_computation | async-start | bytes 16777216 | tf_op jit(solution)/shard_map/all_to_all | solution.py:332
  404.7 0.8 dynamic_slice.13
  405.7 0.8 dynamic-slice_multiply_fusion
  407.2 4.8 multiply_sine_fusion
  412.0 3.1 slice.22
  415.1 2.4 collective-permute-start.1
  417.5 0.8 constant_dynamic-slice_fusion.1
  418.3 0.7 copy.19.shift_ref
  418.9 38.9 %forward_at_0.1.rest_0_ = f32[2,288,128,128]{3,2,1,0:T(8,128)} custom-call(bf16[2,256,256]{2,1,0:T(8,128)(2,1)} %constant.79.table_ref, f32[128,128]{1,0:T(8,128)} %constant.60.clone.cos_ref, f32[128,128]{1,0:T(8,128)} %constant.61.clone.sin_ref, bf16[8,2,128,2048]{3,2,1,0:T(8,128)(2,1)} %all-to-all-done.1.in_ref), custom_call_target="tpu_custom_call" | custom-call | flops 21474836480 | bytes 25165824 | tf_op jit(solution)/shard_map/forward_at_0/pallas_call | solution.py:174
  457.8 72.8 %collective-permute-done.1.in_ref = bf16[8,2,32,2048]{3,2,1,0:T(8,128)(2,1)S(1)} collective-permute-done((bf16[8,2,32,2048]{3,2,1,0:T(8,128)(2,1)}, bf16[8,2,32,2048]{3,2,1,0:T(8,128)(2,1)S(1)}, u32[]{:S(2)}, u32[]{:S(2)}) %collective-permute-start.1) | collective-permute-done | bytes 2097184 | tf_op jit(solution)/shard_map/ppermute | solution.py:336
  530.6 1.3 copy-done.2
  532.0 11.7 %forward_at_16.1.rest_0_ = f32[2,288,128,128]{3,2,1,0:T(8,128)} custom-call(bf16[2,256,256]{2,1,0:T(8,128)(2,1)} %constant.79.table_ref, f32[128,128]{1,0:T(8,128)} %constant.60.clone.cos_ref, f32[128,128]{1,0:T(8,128)} %constant.61.clone.sin_ref, bf16[8,2,32,2048]{3,2,1,0:T(8,128)(2,1)} %copy-done.2, ...), custom_call_target="tpu_custom_call", output_to_operand_aliasing={{}: (4, {})} | custom-call | flops 5368709120 | bytes 6291456 | tf_op jit(solution)/shard_map/forward_at_16/pallas_call | solution.py:174
  543.7 39.0 %forward_at_8.1.spec0.spec1.spec2 = f32[2,288,128,128]{3,2,1,0:T(8,128)} custom-call(bf16[2,256,256]{2,1,0:T(8,128)(2,1)} %constant.79.table_ref, f32[128,128]{1,0:T(8,128)} %constant.60.clone.cos_ref, f32[128,128]{1,0:T(8,128)} %constant.61.clone.sin_ref, bf16[8,2,128,2048]{3,2,1,0:T(8,128)(2,1)} %all-to-all-done.in_ref, ...), custom_call_target="tpu_custom_call", output_to_operand_aliasing={{}: (4, {})} | custom-call | flops 21474836480 | bytes 25165824 | tf_op jit(solution)/shard_map/forward_at_8/pallas_call | solution.py:174
  582.6 111.9 %focus.1 = f32[2,256,16384]{2,1,0:T(8,128)} custom-call(s32[16,8]{1,0:T(8,128)} %copy.19.shift_ref, f32[16,8]{1,0:T(8,128)} %fusion.3.weight_ref, bf16[2,256,256]{2,1,0:T(8,128)(2,1)} %constant.74.table_ref, f32[128,128]{1,0:T(8,128)} %constant.60.clone.cos_ref, f32[128,128]{1,0:T(8,128)} %constant.61.clone.sin_ref, ...), custom_call_target="tpu_custom_call" | custom-call | tf_op jit(solution)/shard_map/focus/pallas_call | solution.py:262
  (21 shorter events, 2.6 us)
Async XLA Ops:
  0.0 405.5 %copy-start = (f32[512,8]{0,1:T(8,128)S(1)}, f32[512,8]{0,1:T(8,128)}, u32[]{:S(2)}) copy-start(f32[512,8]{0,1:T(8,128)} %param.16) | copy-start | bytes 49156
  0.0 185.2 %collective-permute-start = (bf16[2,2048,2048]{2,1,0:T(8,128)(2,1)}, bf16[2,2048,2048]{2,1,0:T(8,128)(2,1)}, u32[]{:S(2)}, u32[]{:S(2)}) collective-permute-start(bf16[2,2048,2048]{2,1,0:T(8,128)(2,1)} %own_ref.3), channel_id=1, source_target_pairs={{1,0},{2,1},{3,2},{5,4},{6,5},{7,6},{9,8},{10,9},{11,10},{13,12},{... | collective-permute-start | bytes 50331656 | tf_op jit(solution)/shard_map/ppermute | solution.py:301
  244.2 130.7 %all-to-all-start.1 = ((bf16[8,2,128,2048]{3,2,1,0:T(8,128)(2,1)}), bf16[8,2,128,2048]{3,2,1,0:T(8,128)(2,1)}, u32[]{:S(2)}, u32[]{:S(2)}) async-start(bf16[8,2,128,2048]{3,2,1,0:T(8,128)(2,1)} %compress_0.1), calls=%async_computation.1 | async-start | bytes 16777216 | tf_op jit(solution)/shard_map/all_to_all | solution.py:332
  374.8 168.8 %all-to-all-start = ((bf16[8,2,128,2048]{3,2,1,0:T(8,128)(2,1)}), bf16[8,2,128,2048]{3,2,1,0:T(8,128)(2,1)}, u32[]{:S(2)}, u32[]{:S(2)}) async-start(bf16[8,2,128,2048]{3,2,1,0:T(8,128)(2,1)} %compress_1.1), calls=%async_computation | async-start | bytes 16777216 | tf_op jit(solution)/shard_map/all_to_all | solution.py:332
  415.1 115.5 %collective-permute-start.1 = (bf16[8,2,32,2048]{3,2,1,0:T(8,128)(2,1)}, bf16[8,2,32,2048]{3,2,1,0:T(8,128)(2,1)S(1)}, u32[]{:S(2)}, u32[]{:S(2)}) collective-permute-start(bf16[8,2,32,2048]{3,2,1,0:T(8,128)(2,1)} %slice.22), channel_id=1, source_target_pairs={{4,0},{8,4},{12,8},{16,12},{20,16},{24,20},{28,24},{1,28},{5,1},{9... | collective-permute-start | bytes 6291464 | tf_op jit(solution)/shard_map/ppermute | solution.py:336
  530.6 1.3 copy-start.2
  582.6 111.9 %copy-start.1 = (f32[512,8]{0,1:T(8,128)S(1)}, f32[512,8]{0,1:T(8,128)}, u32[]{:S(2)}) copy-start(f32[512,8]{0,1:T(8,128)} %param.16) | copy-start | bytes 49156
where the time goes:
time: 696 us; the launch traced here: 695 us
  Pallas kernels  319 us (46%)
  waiting for transfers between devices  316 us (45%)
  starting transfers between devices  40.4 us (6%)
  local copies, waits for them, and re-layouts  10.5 us (2%)
  other arithmetic  8.2 us (1%)
    ppermute x1, waiting for transfers between devices, per_device(): lax.ppermute(echoes[:, :tap_total], 'rg', [(i, i - 1) for i in range(1, r...  177 us
    pallas_call x2, Pallas kernels, compress(): pl.pallas_call(functools.partial(compress_kernel, chunk, block_rows, loca...  118 us
    pallas_call x1, Pallas kernels, focus(): pl.pallas_call(focus_kernel, out_shape=jax.ShapeDtypeStruct((2, local_row...  112 us
    pallas_call x3, Pallas kernels, forward(): pl.pallas_call(forward_kernel, out_shape=jax.ShapeDtypeStruct((2, total_r...  89.5 us
    ppermute x1, waiting for transfers between devices, per_device(): lax.ppermute(turned[0][:, :, :RIM_ROWS], ('az', 'rg'), list(zip(place[1:]...  72.8 us
    all_to_all x2, waiting for transfers between devices, turn(): return lax.all_to_all(part, 'az', split_axis=0, concat_axis=0, tiled=True)  66.2 us
    all_to_all x2, starting transfers between devices, turn(): return lax.all_to_all(part, 'az', split_axis=0, concat_axis=0, tiled=True)  35.4 us
  transfers between devices with their start and end apart: 4, of which 3 were waited for; matrix products, arithmetic and copies ran while one was open for 2% of the time, Pallas kernels for 16%

commit v1 on v0

--- a/solution.py
+++ b/solution.py
@@ -14,7 +14,7 @@
 MAX_SHIFT = 16
 BAND_BINS = 16
 DOPPLER_BLOCKS = 8
-CHUNKS = 2
+COMPRESS_ROWS = 256
 RIM_ROWS = 32
 VMEM = 56 * 1024 * 1024
 
@@ -44,6 +44,7 @@
 
 NN = (((1,), (0,)), ((), ()))
 NT = (((1,), (1,)), ((), ()))
+MESH = pl.DeviceIdType.MESH
 
 
 def mm(a, b, dims):
@@ -59,49 +60,272 @@
     return mm(table[0], high, dims) + (mm(table[1], high, dims) + mm(table[0], low, dims))
 
 
-def compress_kernel(chunk, block_rows, local_rows, w_ref, own_ref, rim_ref, out_ref, window):
-    dest = pl.program_id(1)
-    own_rows = own_ref.shape[1]
-
-    @pl.when(dest == 0)
-    def _():
-        window[:, :own_rows, :] = own_ref[...]
-        window[:, own_rows:, :] = rim_ref[...]
-
-    start = pl.multiple_of(dest * local_rows + chunk * block_rows, block_rows)
+def exchange_kernel(
+    width, block_rows, w_ref, echoes_ref, turned_ref,
+    window, staging, load_sem, rim_send, rim_recv, out_send, out_recv, halo_send
+):
+    az_count, rg_count = lax.axis_size("az"), lax.axis_size("rg")
+    a, g = lax.axis_index("az"), lax.axis_index("rg")
+    last = az_count - 1
+    rows, lines = echoes_ref.shape[1], echoes_ref.shape[2]
+    taps = window.shape[1] - rows
     span = w_ref.shape[2]
-    total = mm(w_ref[0], window[0, pl.ds(start, span), :], NN)
-    total = total + mm(w_ref[1], window[1, pl.ds(start, span), :], NN)
-    total = total.astype(jnp.bfloat16)
-    out_ref[0, 0] = total[:block_rows]
-    out_ref[0, 1] = total[block_rows:]
-
-
-def compress(weights, echoes, rim, chunk, az_count, local_rows):
-    range_dev, lines = echoes.shape[1], echoes.shape[2]
-    taps = rim.shape[1]
-    block_rows = local_rows // CHUNKS
-    tile = math.gcd(512, lines)
+    local_rows = rows // az_count
+    chunks = lines // width
+    has_before, has_after = g > 0, g < rg_count - 1
+    before = lax.rem(g + rg_count - 1, rg_count)
+    after = lax.rem(g + 1, rg_count)
+
+    def columns(c):
+        return pl.ds(pl.multiple_of(c * width, width), width)
+
+    def own_load(c):
+        return pltpu.make_async_copy(
+            echoes_ref.at[:, :, columns(c)],
+            window.at[:, pl.ds(0, rows), columns(c)],
+            load_sem.at[c],
+        )
+
+    def rim_copy(c):
+        return pltpu.make_async_remote_copy(
+            src_ref=echoes_ref.at[:, pl.ds(0, taps), columns(c)],
+            dst_ref=window.at[:, pl.ds(rows, taps), columns(c)],
+            send_sem=rim_send.at[c],
+            recv_sem=rim_recv.at[c],
+            device_id=(a, before),
+            device_id_type=MESH,
+        )
+
+    def start_load(c, _):
+        own_load(c).start()
+        return 0
+
+    lax.fori_loop(0, chunks, start_load, 0)
+
+    barrier = pltpu.get_barrier_semaphore()
+
+    def greet(az_at, rg_at):
+        pl.semaphore_signal(barrier, inc=1, device_id=(az_at, rg_at), device_id_type=MESH)
+
+    def greet_peer(d, _):
+        greet(lax.rem(a + d, az_count), g)
+        return 0
+
+    lax.fori_loop(1, az_count, greet_peer, 0)
+
+    @pl.when(has_before)
+    def _():
+        greet(a, before)
+
+    @pl.when(has_after)
+    def _():
+        greet(a, after)
+
+    @pl.when(has_before & (a != last))
+    def _():
+        greet(last, before)
+
+    @pl.when(has_after & (a == last))
+    def _():
+        def greet_halo(b, _):
+            greet(b, after)
+            return 0
+
+        lax.fori_loop(0, last, greet_halo, 0)
+
+    one = lambda flag: jnp.where(flag, 1, 0)
+    pl.semaphore_wait(
+        barrier,
+        last
+        + one(has_before)
+        + one(has_after)
+        + one(has_before & (a != last))
+        + last * one(has_after & (a == last)),
+    )
+
+    upfront = jnp.where(lax.rem(g, 2) == 1, chunks, min(2, chunks))
+
+    @pl.when(has_before)
+    def _():
+        def start_rim(c, _):
+            rim_copy(c).start()
+            return 0
+
+        lax.fori_loop(0, upfront, start_rim, 0)
+
+    @pl.when(jnp.logical_not(has_after))
+    def _():
+        def clear(i, _):
+            at = pl.ds(pl.multiple_of(rows + i * 128, 128), 128)
+            window[:, at, :] = jnp.zeros((2, 128, lines), window.dtype)
+            return 0
+
+        lax.fori_loop(0, taps // 128, clear, 0)
+
+        @pl.when(a == last)
+        def _():
+            staging[:, rows:, :] = jnp.zeros((2, RIM_ROWS, lines), staging.dtype)
+
+            def clear_halo(b, _):
+                pltpu.make_async_copy(
+                    staging.at[:, pl.ds(rows, RIM_ROWS), :],
+                    turned_ref.at[b, :, pl.ds(local_rows, RIM_ROWS), :],
+                    out_recv.at[b],
+                ).start()
+                return 0
+
+            lax.fori_loop(0, az_count, clear_halo, 0)
+
+    def block_copy(b, height, cols):
+        return pltpu.make_async_remote_copy(
+            src_ref=staging.at[:, pl.ds(pl.multiple_of(b * local_rows, local_rows), height), cols],
+            dst_ref=turned_ref.at[a, :, pl.ds(0, height), cols],
+            send_sem=out_send.at[b],
+            recv_sem=out_recv.at[a],
+            device_id=(b, g),
+            device_id_type=MESH,
+        )
+
+    def own_copy(height, cols):
+        return pltpu.make_async_copy(
+            staging.at[:, pl.ds(pl.multiple_of(a * local_rows, local_rows), height), cols],
+            turned_ref.at[a, :, pl.ds(0, height), cols],
+            out_recv.at[a],
+        )
+
+    def halo_copy(cols):
+        return pltpu.make_async_remote_copy(
+            src_ref=staging.at[:, pl.ds(0, RIM_ROWS), cols],
+            dst_ref=turned_ref.at[a, :, pl.ds(local_rows, RIM_ROWS), cols],
+            send_sem=halo_send.at[0],
+            recv_sem=out_recv.at[a],
+            device_id=(last, before),
+            device_id_type=MESH,
+        )
+
+    tall = local_rows + RIM_ROWS
+
+    def chunk(c, _):
+        cols = columns(c)
+        own_load(c).wait()
+
+        @pl.when(has_after)
+        def _():
+            rim_copy(c).wait_recv()
+
+        def block(i, _):
+            start = pl.multiple_of(i * block_rows, block_rows)
+            total = mm(w_ref[0], window[0, pl.ds(start, span), cols], NN)
+            total = total + mm(w_ref[1], window[1, pl.ds(start, span), cols], NN)
+            total = total.astype(jnp.bfloat16)
+            staging[0, pl.ds(start, block_rows), cols] = total[:block_rows]
+            staging[1, pl.ds(start, block_rows), cols] = total[block_rows:]
+            return 0
+
+        lax.fori_loop(0, rows // block_rows, block, 0)
+
+        def send(d, _):
+            b = lax.rem(a + d, az_count)
+
+            @pl.when(b == last)
+            def _():
+                block_copy(b, local_rows, cols).start()
+
+            @pl.when(b != last)
+            def _():
+                block_copy(b, tall, cols).start()
+
+            return 0
+
+        lax.fori_loop(1, az_count, send, 0)
+
+        @pl.when(a == last)
+        def _():
+            own_copy(local_rows, cols).start()
+
+        @pl.when(a != last)
+        def _():
+            own_copy(tall, cols).start()
+
+        @pl.when(has_before)
+        def _():
+            halo_copy(cols).start()
+            rim_copy(c).wait_send()
+
+            @pl.when(c + upfront < chunks)
+            def _():
+                rim_copy(c + upfront).start()
+
+        return 0
+
+    lax.fori_loop(0, chunks, chunk, 0)
+
+    every = pl.ds(0, lines)
+
+    def finish_send(d, _):
+        b = lax.rem(a + d, az_count)
+
+        @pl.when(b == last)
+        def _():
+            block_copy(b, local_rows, every).wait_send()
+
+        @pl.when(b != last)
+        def _():
+            block_copy(b, tall, every).wait_send()
+
+        return 0
+
+    lax.fori_loop(1, az_count, finish_send, 0)
+
+    @pl.when(has_before)
+    def _():
+        halo_copy(every).wait_send()
+
+    def finish_receive(b, _):
+        pltpu.make_async_copy(turned_ref.at[b], turned_ref.at[b], out_recv.at[b]).wait()
+        return 0
+
+    lax.fori_loop(0, az_count, finish_receive, 0)
+
+
+def exchange(weights, echoes, az_count):
+    rows, lines = echoes.shape[1], echoes.shape[2]
     span = weights.shape[2]
+    block_rows = weights.shape[1] // 2
+    taps = span - block_rows
+    width = math.gcd(256, lines)
+    chunks = lines // width
+    local_rows = rows // az_count
     return pl.pallas_call(
-        functools.partial(compress_kernel, chunk, block_rows, local_rows),
-        out_shape=jax.ShapeDtypeStruct((az_count, 2, block_rows, lines), jnp.bfloat16),
-        grid=(lines // tile, az_count),
+        functools.partial(exchange_kernel, width, block_rows),
+        out_shape=jax.ShapeDtypeStruct(
+            (az_count, 2, local_rows + RIM_ROWS, lines), jnp.bfloat16
+        ),
         in_specs=[
-            pl.BlockSpec(weights.shape, lambda l, j: (0, 0, 0)),
-            pl.BlockSpec((2, range_dev, tile), lambda l, j: (0, 0, l)),
-            pl.BlockSpec((2, taps, tile), lambda l, j: (0, 0, l)),
+            pl.BlockSpec(memory_space=pltpu.VMEM),
+            pl.BlockSpec(memory_space=pl.ANY),
         ],
-        out_specs=pl.BlockSpec((1, 2, block_rows, tile), lambda l, j: (j, 0, 0, l)),
-        scratch_shapes=[pltpu.VMEM((2, range_dev + taps, tile), jnp.bfloat16)],
-        compiler_params=pltpu.CompilerParams(vmem_limit_bytes=VMEM),
+        out_specs=pl.BlockSpec(memory_space=pl.ANY),
+        scratch_shapes=[
+            pltpu.VMEM((2, rows + taps, lines), jnp.bfloat16),
+            pltpu.VMEM((2, rows + RIM_ROWS, lines), jnp.bfloat16),
+            pltpu.SemaphoreType.DMA((chunks,)),
+            pltpu.SemaphoreType.DMA((chunks,)),
+            pltpu.SemaphoreType.DMA((chunks,)),
+            pltpu.SemaphoreType.DMA((az_count,)),
+            pltpu.SemaphoreType.DMA((az_count,)),
+            pltpu.SemaphoreType.DMA((1,)),
+        ],
+        compiler_params=pltpu.CompilerParams(
+            vmem_limit_bytes=60 * 1024 * 1024, collective_id=0, has_side_effects=True
+        ),
         cost_estimate=pl.CostEstimate(
-            flops=8 * az_count * block_rows * span * lines,
-            bytes_accessed=4 * lines * (2 * range_dev + taps),
+            flops=8 * rows * span * lines,
+            bytes_accessed=4 * lines * (4 * rows + taps),
             transcendentals=0,
         ),
-        name=f"compress_{chunk}",
-    )(weights, echoes, rim)
+        name="exchange",
+    )(weights, echoes)
 
 
 def compress_weights(replica, block_rows):
@@ -288,19 +512,15 @@
 
 
 def per_device(echoes, replica, shifts, tap_counts, interp_weights, fm_rates):
-    tap_total = replica.shape[1]
     range_dev = echoes.shape[1]
     az_count = lax.axis_size("az")
     rg_count = lax.axis_size("rg")
     local_rows = range_dev // az_count
-    block_rows = local_rows // CHUNKS
+    block_rows = COMPRESS_ROWS
     bands_here = local_rows // BAND_BINS
     az_pos = lax.axis_index("az")
     rg_pos = lax.axis_index("rg")
 
-    rim = lax.ppermute(
-        echoes[:, :tap_total], "rg", [(i, i - 1) for i in range(1, rg_count)]
-    )
     weights = compress_weights(replica, block_rows)
     forward_m, inverse_m, twist_cos, twist_sin = transform_tables()
     cosine = jnp.asarray(twist_cos, jnp.float32)
@@ -327,21 +547,9 @@
     pcos = jnp.cos(phases)
     psin = jnp.sin(phases)
 
-    def turn(chunk):
-        part = compress(weights, echoes, rim, chunk, az_count, local_rows)
-        return lax.all_to_all(part, "az", split_axis=0, concat_axis=0, tiled=True)
-
-    turned = [turn(chunk) for chunk in range(CHUNKS)]
-    place = [a * rg_count + g for g in range(rg_count) for a in range(az_count)]
-    beyond = lax.ppermute(
-        turned[0][:, :, :RIM_ROWS], ("az", "rg"), list(zip(place[1:], place[:-1]))
-    )
+    turned = exchange(weights, echoes, az_count)
     total_rows = local_rows + RIM_ROWS
-    step = block_rows // BAND_BINS
-    spectrum = forward(forward_tables, turned[0], None, 0, total_rows)
-    spectrum = forward(forward_tables, beyond, spectrum, CHUNKS * step, total_rows)
-    for chunk in range(1, CHUNKS):
-        spectrum = forward(forward_tables, turned[chunk], spectrum, chunk * step, total_rows)
+    spectrum = forward(forward_tables, turned, None, 0, total_rows)
     return focus(band_shift, live_weight, inverse_tables, pcos, psin, spectrum, local_rows)
 
 

time: 696 us -> 647 us (0.930)
  waiting for transfers between devices: 316 us -> 0 us
  Pallas kernels: 319 us -> 622 us
  starting transfers between devices: 40.4 us -> 0 us
    pallas_call x2 -> x1, Pallas kernels: 118 us -> 425 us  [exchange(): pl.pallas_call(functools.partial(exchange_kernel, width, block_rows), out...]
    ppermute x2 -> x0, waiting for transfers between devices: 250 us -> none  [the longest x1 177 us: per_device(): lax.ppermute(echoes[:, :tap_total], 'rg', [(i, i - 1) for i in range(1, r...]
    all_to_all x2 -> x0, waiting for transfers between devices: 66.2 us -> none  [turn(): return lax.all_to_all(part, 'az', split_axis=0, concat_axis=0, tiled=True)]
    all_to_all x2 -> x0, starting transfers between devices: 35.4 us -> none  [turn(): return lax.all_to_all(part, 'az', split_axis=0, concat_axis=0, tiled=True)]
    pallas_call x3 -> x1, Pallas kernels: 89.5 us -> 84.3 us  [forward(): pl.pallas_call(forward_kernel, out_shape=jax.ShapeDtypeStruct((2, total_r...]
  transfers between devices with their start and end apart: 4 -> 0, of which waited for: 3 -> 0; matrix products, arithmetic and copies ran while one was open for 2% -> 0% of each run, Pallas kernels for 16% -> 0%
where the time goes in v1:
time: 647 us; the launch traced here: 644 us
  Pallas kernels  622 us (96%)
  local copies, waits for them, and re-layouts  12.8 us (2%)
  other arithmetic  9.51 us (1%)
    pallas_call x1, Pallas kernels, exchange(): pl.pallas_call(functools.partial(exchange_kernel, width, block_rows), out...  425 us
    pallas_call x1, Pallas kernels, focus(): pl.pallas_call(focus_kernel, out_shape=jax.ShapeDtypeStruct((2, local_row...  112 us
    pallas_call x1, Pallas kernels, forward(): pl.pallas_call(forward_kernel, out_shape=jax.ShapeDtypeStruct((2, total_r...  84.3 us

profile of v1, /device:TPU:29, one launch (start us, length us, event | category | flops | bytes accessed | tf_op | source)
XLA Modules:
  0.0 644.1 jit_solution(7203979554829746695)
XLA Ops:
  0.0 0.8 dynamic_slice.13
  0.8 0.8 dynamic-slice_multiply_fusion
  1.5 0.1 constant_dynamic-slice_fusion.1
  1.6 0.8 constant_dynamic-slice_fusion
  2.4 0.1 copy.18
  2.4 0.7 fusion.3.weight_ref
  3.1 0.7 copy.17.shift_ref
  3.8 0.8 slice_reduce_fusion
  4.6 0.1 fusion.2
  4.7 0.1 tile.8
  4.8 1.6 tile.9
  6.5 0.1 slice.16
  6.6 2.2 reshape.30
  8.7 0.1 tile.20
  8.8 1.6 tile.21
  10.5 1.1 slice.17
  11.6 2.8 reshape.31
  14.4 0.2 neg.3
  14.6 0.4 maximum_bitcast_fusion
  15.0 2.6 pad_maximum_fusion.w_ref
  17.6 4.8 multiply_sine_fusion
  22.4 425.5 %exchange.1.in_ref = bf16[8,2,288,2048]{3,2,1,0:T(8,128)(2,1)} custom-call(bf16[2,512,2304]{2,1,0:T(8,128)(2,1)} %pad_maximum_fusion.w_ref, bf16[2,2048,2048]{2,1,0:T(8,128)(2,1)} %echoes_ref.1), custom_call_target="tpu_custom_call" | custom-call | flops 77309411328 | bytes 83886080 | tf_op jit(solution)/shard_map/exchange/pallas_call | solution.py:299
  447.9 84.3 %forward_at_0.1.spec0.spec1.spec2 = f32[2,288,128,128]{3,2,1,0:T(8,128)} custom-call(bf16[2,256,256]{2,1,0:T(8,128)(2,1)} %constant.79.table_ref, f32[128,128]{1,0:T(8,128)} %constant.60.clone.cos_ref, f32[128,128]{1,0:T(8,128)} %constant.61.clone.sin_ref, bf16[8,2,288,2048]{3,2,1,0:T(8,128)(2,1)} %exchange.1.in_ref), custom_call_target="tpu_custom_call" | custom-call | flops 48318382080 | bytes 56623104 | tf_op jit(solution)/shard_map/forward_at_0/pallas_call | solution.py:398
  532.2 111.9 %focus.1 = f32[2,256,16384]{2,1,0:T(8,128)} custom-call(s32[16,8]{1,0:T(8,128)} %copy.17.shift_ref, f32[16,8]{1,0:T(8,128)} %fusion.3.weight_ref, bf16[2,256,256]{2,1,0:T(8,128)(2,1)} %constant.74.table_ref, f32[128,128]{1,0:T(8,128)} %constant.60.clone.cos_ref, f32[128,128]{1,0:T(8,128)} %constant.61.clone.sin_ref, ...), custom_call_target="tpu_custom_call" | custom-call | tf_op jit(solution)/shard_map/focus/pallas_call | solution.py:486
  (9 shorter events, 0.0 us)
Async XLA Ops:
  0.0 1.5 copy-start
  11.6 3.0 copy-start.2
  532.2 111.9 %copy-start.1 = (s32[512,8]{0,1:T(8,128)S(1)}, s32[512,8]{0,1:T(8,128)}, u32[]{:S(2)}) copy-start(s32[512,8]{0,1:T(8,128)} %param.14) | copy-start | bytes 49156

commit v2 on v1

v2 whole, which is shorter than its diff:
```python
import functools
import math

import jax
import jax.numpy as jnp
import numpy as np
from jax import lax
from jax.experimental import pallas as pl
from jax.experimental.pallas import tpu as pltpu
from jax.sharding import PartitionSpec as P

SIDE = 128
INTERP_TAPS = 8
MAX_SHIFT = 16
BAND_BINS = 16
DOPPLER_BLOCKS = 8
COMPRESS_ROWS = 256
RIM_ROWS = 32
VMEM = 56 * 1024 * 1024


def transform_tables():
    k = np.arange(SIDE)
    angle = 2.0 * np.pi * ((k[:, None] * k[None, :]) % SIDE) / SIDE
    c, s = np.cos(angle), np.sin(angle)
    forward = np.block([[c, s], [-s, c]])
    inverse = np.block([[c, -s], [s, c]])
    twist = 2.0 * np.pi * (k[:, None] * k[None, :]) / (SIDE * SIDE)
    return forward, inverse, np.cos(twist), np.sin(twist)


def split_const(matrix):
    high = jnp.asarray(matrix, jnp.float32).astype(jnp.bfloat16)
    low_np = np.asarray(matrix, np.float64) - np.asarray(
        np.asarray(matrix, np.float32).astype(jnp.bfloat16), np.float64
    )
    return jnp.stack([high, jnp.asarray(low_np, jnp.float32).astype(jnp.bfloat16)])


def split_data(value):
    high = value.astype(jnp.bfloat16)
    return high, (value - high.astype(jnp.float32)).astype(jnp.bfloat16)


NN = (((1,), (0,)), ((), ()))
NT = (((1,), (1,)), ((), ()))
MESH = pl.DeviceIdType.MESH


def mm(a, b, dims):
    return lax.dot_general(a, b, dims, preferred_element_type=jnp.float32)


def mm2(table, data, dims):
    return mm(table[0], data, dims) + mm(table[1], data, dims)


def mm3(table, value, dims):
    high, low = split_data(value)
    return mm(table[0], high, dims) + (mm(table[1], high, dims) + mm(table[0], low, dims))


def phase_starts(bands):
    cuts = [0, max(2, bands * 6 // 16), bands * 11 // 16, bands * 14 // 16]
    return [at for k, at in enumerate(cuts) if k == 0 or at > cuts[k - 1]] + [bands]


def exchange_kernel(
    width, block_rows,
    shift_ref, weight_ref, w_ref, ftable_ref, itable_ref, cos_ref, sin_ref, pcos_ref, psin_ref,
    echoes_ref, turned_ref, inner_ref,
    window, arrived, data, spectrum, moved, staged,
    load_sem, rim_send, rim_recv, out_send, out_recv, halo_send, halo_recv, in_sem, inner_sem, token,
):
    az_count, rg_count = lax.axis_size("az"), lax.axis_size("rg")
    a, g = lax.axis_index("az"), lax.axis_index("rg")
    last, middle = az_count - 1, az_count // 2 - 1
    rows, lines = echoes_ref.shape[1], echoes_ref.shape[2]
    taps = window.shape[1] - rows
    span = w_ref.shape[2]
    local_rows = rows // az_count
    bands = local_rows // BAND_BINS
    starts = phase_starts(bands)
    phases = len(starts) - 1
    chunks = lines // width
    has_before, has_after = g > 0, g < rg_count - 1
    before = lax.rem(g + rg_count - 1, rg_count)
    after = lax.rem(g + 1, rg_count)
    late = lax.rem(g, 2) == 1
    early = jnp.logical_not(late)
    whole_rows, whole_lines = pl.ds(0, local_rows), pl.ds(0, lines)
    halo_rows = pl.ds(local_rows, RIM_ROWS)

    def columns(c):
        return pl.ds(pl.multiple_of(c * width, width), width)

    def own_load(c):
        return pltpu.make_async_copy(
            echoes_ref.at[:, :, columns(c)],
            window.at[:, pl.ds(0, rows), columns(c)],
            load_sem.at[c],
        )

    def rim_copy(c):
        return pltpu.make_async_remote_copy(
            src_ref=echoes_ref.at[:, pl.ds(0, taps), columns(c)],
            dst_ref=window.at[:, pl.ds(rows, taps), columns(c)],
            send_sem=rim_send.at[c],
            recv_sem=rim_recv.at[c],
            device_id=(a, before),
            device_id_type=MESH,
        )

    def start_load(c, _):
        own_load(c).start()
        return 0

    lax.fori_loop(0, chunks, start_load, 0)

    barrier = pltpu.get_barrier_semaphore()

    def greet(az_at, rg_at):
        pl.semaphore_signal(barrier, inc=1, device_id=(az_at, rg_at), device_id_type=MESH)

    def greet_peer(d, _):
        greet(lax.rem(a + d, az_count), g)
        return 0

    lax.fori_loop(1, az_count, greet_peer, 0)

    @pl.when(has_before)
    def _():
        greet(a, before)

    @pl.when(has_after)
    def _():
        greet(a, after)

    @pl.when(has_before & (a != last))
    def _():
        greet(last, before)

    @pl.when(has_after & (a == last))
    def _():
        def greet_halo(b, _):
            greet(b, after)
            return 0

        lax.fori_loop(0, last, greet_halo, 0)

    one = lambda flag: jnp.where(flag, 1, 0)
    pl.semaphore_wait(
        barrier,
        last
        + one(has_before)
        + one(has_after)
        + one(has_before & (a != last))
        + last * one(has_after & (a == last)),
    )

    upfront = jnp.where(late, chunks, min(2, chunks))

    @pl.when(has_before)
    def _():
        def start_rim(c, _):
            rim_copy(c).start()
            return 0

        lax.fori_loop(0, upfront, start_rim, 0)

    @pl.when(jnp.logical_not(has_after))
    def _():
        def clear(i, _):
            at = pl.ds(pl.multiple_of(rows + i * 128, 128), 128)
            window[:, at, :] = jnp.zeros((2, 128, lines), window.dtype)
            return 0

        lax.fori_loop(0, taps // 128, clear, 0)

        @pl.when(a == last)
        def _():
            def clear_halo(b, _):
                pltpu.make_async_copy(
                    window.at[:, pl.ds(rows, RIM_ROWS), :],
                    turned_ref.at[b, :, halo_rows, :],
                    halo_recv.at[0],
                ).start()
                return 0

            lax.fori_loop(0, az_count, clear_halo, 0)

    def rows_of(b, first, height):
        return pl.ds(pl.multiple_of(b * local_rows + first, BAND_BINS), height)

    def block_copy(b, first, height, cols, send, receive):
        return pltpu.make_async_remote_copy(
            src_ref=window.at[:, rows_of(b, first, height), cols],
            dst_ref=turned_ref.at[a, :, pl.ds(first, height), cols],
            send_sem=out_send.at[send],
            recv_sem=out_recv.at[receive],
            device_id=(b, g),
            device_id_type=MESH,
        )

    def send_blocks(first, height, cols, send, receive):
        def one_block(d, _):
            block_copy(lax.rem(a + d, az_count), first, height, cols, send, receive).start()
            return 0

        lax.fori_loop(1, az_count, one_block, 0)
        pltpu.make_async_copy(
            window.at[:, rows_of(a, first, height), cols],
            turned_ref.at[a, :, pl.ds(first, height), cols],
            out_recv.at[receive],
        ).start()

    def sent_blocks(height, cols, send):
        held = window.at[:, pl.ds(0, last * height), cols]
        pltpu.make_async_copy(held, held, out_send.at[send]).wait()

    def halo_copy(first, az_at, rg_at, send):
        return pltpu.make_async_remote_copy(
            src_ref=window.at[:, pl.ds(first, RIM_ROWS), :],
            dst_ref=turned_ref.at[a, :, halo_rows, :],
            send_sem=halo_send.at[send],
            recv_sem=halo_recv.at[0],
            device_id=(az_at, rg_at),
            device_id_type=MESH,
        )

    middle_halo = halo_copy((middle + 1) * local_rows, middle, g, 0)
    outer_halo = halo_copy(0, last, before, 1)
    neighbour_halo = pltpu.make_async_remote_copy(
        src_ref=turned_ref.at[:, :, pl.ds(0, RIM_ROWS), :],
        dst_ref=turned_ref.at[:, :, halo_rows, :],
        send_sem=halo_send.at[2],
        recv_sem=halo_recv.at[0],
        device_id=(lax.rem(a + last, az_count), g),
        device_id_type=MESH,
    )
    passes_halo = (a > 0) & (a != middle + 1)

    def chunk(c, _):
        cols = columns(c)
        own_load(c).wait()

        @pl.when(has_after)
        def _():
            rim_copy(c).wait_recv()

        def block(i, _):
            start = pl.multiple_of(i * block_rows, block_rows)
            total = mm(w_ref[0], window[0, pl.ds(start, span), cols], NN)
            total = total + mm(w_ref[1], window[1, pl.ds(start, span), cols], NN)
            total = total.astype(jnp.bfloat16)
            window[0, pl.ds(start, block_rows), cols] = total[:block_rows]
            window[1, pl.ds(start, block_rows), cols] = total[block_rows:]
            return 0

        lax.fori_loop(0, rows // block_rows, block, 0)

        @pl.when(early)
        def _():
            send_blocks(0, local_rows, cols, c, 0)

        @pl.when(has_before)
        def _():
            rim_copy(c).wait_send()

            @pl.when(c + upfront < chunks)
            def _():
                rim_copy(c + upfront).start()

        return 0

    lax.fori_loop(0, chunks, chunk, 0)

    @pl.when(a == middle)
    def _():
        pltpu.make_async_copy(
            window.at[:, pl.ds((middle + 1) * local_rows, RIM_ROWS), :],
            turned_ref.at[a, :, halo_rows, :],
            halo_recv.at[0],
        ).start()

    @pl.when(a != middle)
    def _():
        middle_halo.start()

    @pl.when(has_before)
    def _():
        outer_halo.start()

    def send_phase(p):
        send_blocks(starts[p] * BAND_BINS, height_of(p), whole_lines, p, p)

    def height_of(p):
        return (starts[p + 1] - starts[p]) * BAND_BINS

    @pl.when(early)
    def _():
        def sent_chunk(c, _):
            sent_blocks(local_rows, columns(c), 0 + c)
            return 0

        lax.fori_loop(0, chunks - 1, sent_chunk, 0)
        pl.semaphore_signal(token, inc=1, device_id=(a, after), device_id_type=MESH)
        sent_chunk(chunks - 1, 0)
        pltpu.make_async_copy(
            turned_ref.at[:, :, whole_rows, :], turned_ref.at[:, :, whole_rows, :], out_recv.at[0]
        ).wait()

    @pl.when(late)
    def _():
        pl.semaphore_wait(token, 1)
        send_phase(0)
        if phases > 1:
            send_phase(1)

    def enter_phase(p):
        @pl.when(late)
        def _():
            sent_blocks(height_of(p), whole_lines, p)
            if p + 2 < phases:
                send_phase(p + 2)
            landed = turned_ref.at[:, :, pl.ds(starts[p] * BAND_BINS, height_of(p)), :]
            pltpu.make_async_copy(landed, landed, out_recv.at[p]).wait()

    total_bands = bands + RIM_ROWS // BAND_BINS
    fresh = RIM_ROWS

    def band_load(i):
        slot = lax.rem(i, 2)
        return pltpu.make_async_copy(
            turned_ref.at[:, :, pl.ds(pl.multiple_of(i * BAND_BINS, BAND_BINS), BAND_BINS), :],
            arrived.at[slot],
            in_sem.at[slot],
        )

    def inner_store(band):
        slot = lax.rem(band, 2)
        return pltpu.make_async_copy(
            staged.at[slot],
            inner_ref.at[pl.ds(pl.multiple_of(band * BAND_BINS, BAND_BINS), BAND_BINS)],
            inner_sem.at[slot],
        )

    def band_step(i, _):
        for p in range(phases):
            @pl.when(i == starts[p])
            def _():
                enter_phase(p)
                if p == 0:
                    @pl.when(passes_halo)
                    def _():
                        neighbour_halo.start()
                band_load(i).start()

        @pl.when(i == bands)
        def _():
            whole_halo = turned_ref.at[:, :, halo_rows, :]
            pltpu.make_async_copy(whole_halo, whole_halo, halo_recv.at[0]).wait()
            band_load(i).start()

        band_load(i).wait()
        opens = i + 1 == total_bands
        for at in starts:
            opens = opens | (i + 1 == at)

        @pl.when(jnp.logical_not(opens))
        def _():
            band_load(i + 1).start()

        forward_band(lax.rem(i, 2), ftable_ref, cos_ref, sin_ref, arrived, data, spectrum, fresh)

        @pl.when(i >= 2)
        def _():
            band = i - 2

            @pl.when(band >= 2)
            def _():
                inner_store(band - 2).wait()

            migrate_band(
                band, shift_ref, weight_ref, itable_ref, cos_ref, sin_ref, pcos_ref, psin_ref,
                spectrum, moved, staged, lax.rem(band, 2),
            )
            inner_store(band).start()

        def slide(r, _):
            spectrum[:, r] = spectrum[:, r + BAND_BINS]
            return 0

        lax.fori_loop(0, fresh, slide, 0)
        return 0

    lax.fori_loop(0, total_bands, band_step, 0)
    for band in range(max(0, bands - 2), bands):
        inner_store(band).wait()

    @pl.when(a != middle)
    def _():
        middle_halo.wait_send()

    @pl.when(has_before)
    def _():
        outer_halo.wait_send()

    @pl.when(passes_halo)
    def _():
        neighbour_halo.wait_send()


def forward_band(slot, table_ref, cos_ref, sin_ref, arrived, data, spectrum, fresh):
    _, az_count, _, rows, lines = arrived.shape
    per = lines // SIDE
    for source in range(az_count):
        for c in range(2):
            piece = arrived[slot, source, c].astype(jnp.float32)
            data[:, c * SIDE + source * per : c * SIDE + (source + 1) * per, :] = piece.reshape(
                rows, per, SIDE
            )

    def pair(i, _):
        both = jnp.concatenate([data[2 * i], data[2 * i + 1]], axis=1).astype(jnp.bfloat16)
        first = mm2(table_ref, both, NN)
        cosine, sine = cos_ref[...], sin_ref[...]
        turned = []
        for k in range(2):
            real = first[:SIDE, k * SIDE : (k + 1) * SIDE]
            imag = first[SIDE:, k * SIDE : (k + 1) * SIDE]
            turned.append(
                jnp.concatenate(
                    [real * cosine + imag * sine, imag * cosine - real * sine], axis=1
                )
            )
        second = mm3(table_ref, jnp.concatenate(turned, axis=0), NT)
        for k in range(2):
            spectrum[0, fresh + 2 * i + k] = second[:SIDE, k * SIDE : (k + 1) * SIDE]
            spectrum[1, fresh + 2 * i + k] = second[SIDE:, k * SIDE : (k + 1) * SIDE]
        return 0

    lax.fori_loop(0, rows // 2, pair, 0, unroll=2)


def migrate_band(
    band, shift_ref, weight_ref, table_ref, cos_ref, sin_ref, pcos_ref, psin_ref,
    window, moved, staged, slot
):
    deep = SIDE // DOPPLER_BLOCKS
    taps = [weight_ref[band, t] for t in range(INTERP_TAPS)]

    def block(d, _):
        shift = shift_ref[band, d]
        spot = pl.ds(pl.multiple_of(d * deep, deep), deep)
        pcos, psin = pcos_ref[band, spot, :], psin_ref[band, spot, :]
        for half in range(2):
            rows = BAND_BINS // 2
            parts = []
            for c in range(2):
                total = taps[0] * window[c, pl.ds(shift + half * rows, rows), spot, :]
                for t in range(1, INTERP_TAPS):
                    total = total + taps[t] * window[c, pl.ds(shift + half * rows + t, rows), spot, :]
                parts.append(total)
            real, imag = parts
            put = slice(half * rows, (half + 1) * rows)
            moved[put, spot, :] = real * pcos + imag * psin
            low = pl.ds(pl.multiple_of(SIDE + d * deep, deep), deep)
            moved[put, low, :] = imag * pcos - real * psin
        return 0

    lax.fori_loop(0, DOPPLER_BLOCKS, block, 0)

    def pair(i, _):
        both = jnp.concatenate([moved[2 * i], moved[2 * i + 1]], axis=1)
        first = mm3(table_ref, both, NN)
        cosine, sine = cos_ref[...], sin_ref[...]
        for k in range(2):
            real = first[:SIDE, k * SIDE : (k + 1) * SIDE]
            imag = first[SIDE:, k * SIDE : (k + 1) * SIDE]
            staged[slot, 2 * i + k, :, :SIDE] = (real * cosine - imag * sine).astype(jnp.bfloat16)
            staged[slot, 2 * i + k, :, SIDE:] = (imag * cosine + real * sine).astype(jnp.bfloat16)
        return 0

    lax.fori_loop(0, BAND_BINS // 2, pair, 0, unroll=2)


def exchange(shifts, live_weight, weights, ftables, itable, pcos, psin, echoes, az_count):
    ftable, cosine, sine = ftables
    rows, lines = echoes.shape[1], echoes.shape[2]
    span = weights.shape[2]
    block_rows = weights.shape[1] // 2
    taps = span - block_rows
    width = math.gcd(256, lines)
    chunks = lines // width
    local_rows = rows // az_count
    phases = len(phase_starts(local_rows // BAND_BINS)) - 1
    vmem = pl.BlockSpec(memory_space=pltpu.VMEM)
    smem = pl.BlockSpec(memory_space=pltpu.SMEM)
    anywhere = pl.BlockSpec(memory_space=pl.ANY)
    dma = pltpu.SemaphoreType.DMA
    return pl.pallas_call(
        functools.partial(exchange_kernel, width, block_rows),
        out_shape=[
            jax.ShapeDtypeStruct((az_count, 2, local_rows + RIM_ROWS, lines), jnp.bfloat16),
            jax.ShapeDtypeStruct((local_rows, SIDE, 2 * SIDE), jnp.bfloat16),
        ],
        in_specs=[smem, smem] + [vmem] * 7 + [anywhere],
        out_specs=[anywhere, anywhere],
        scratch_shapes=[
            pltpu.VMEM((2, rows + taps, lines), jnp.bfloat16),
            pltpu.VMEM((2, az_count, 2, BAND_BINS, lines), jnp.bfloat16),
            pltpu.VMEM((BAND_BINS, 2 * SIDE, SIDE), jnp.float32),
            pltpu.VMEM((2, RIM_ROWS + BAND_BINS, SIDE, SIDE), jnp.float32),
            pltpu.VMEM((BAND_BINS, 2 * SIDE, SIDE), jnp.float32),
            pltpu.VMEM((2, BAND_BINS, SIDE, 2 * SIDE), jnp.bfloat16),
            dma((chunks,)),
            dma((chunks,)),
            dma((chunks,)),
            dma((max(chunks, phases),)),
            dma((phases,)),
            dma((3,)),
            dma((1,)),
            dma((2,)),
            dma((2,)),
            pltpu.SemaphoreType.REGULAR,
        ],
        compiler_params=pltpu.CompilerParams(
            vmem_limit_bytes=60 * 1024 * 1024, collective_id=0, has_side_effects=True
        ),
        cost_estimate=pl.CostEstimate(
            flops=8 * rows * span * lines + local_rows * 8 * 16 * SIDE**3,
            bytes_accessed=4 * lines * (4 * rows + taps),
            transcendentals=0,
        ),
        name="exchange",
    )(shifts, live_weight, weights, ftable, itable, cosine, sine, pcos, psin, echoes)


def finish_kernel(table_ref, inner_ref, out_ref, image):
    def pair(i, _):
        both = jnp.concatenate([inner_ref[2 * i], inner_ref[2 * i + 1]], axis=0)
        second = mm2(table_ref, both, NT) * (1.0 / (SIDE * SIDE))
        for k in range(2):
            image[2 * i + k] = second[:, k * SIDE : (k + 1) * SIDE]
        return 0

    lax.fori_loop(0, BAND_BINS // 2, pair, 0, unroll=2)
    group = 16
    for c in range(2):
        for g in range(SIDE // group):
            piece = image[:, c * SIDE + g * group : c * SIDE + (g + 1) * group, :]
            out_ref[c, :, g * group * SIDE : (g + 1) * group * SIDE] = piece.reshape(
                BAND_BINS, group * SIDE
            )


def finish(table, inner):
    local_rows = inner.shape[0]
    return pl.pallas_call(
        finish_kernel,
        out_shape=jax.ShapeDtypeStruct((2, local_rows, SIDE * SIDE), jnp.float32),
        grid=(local_rows // BAND_BINS,),
        in_specs=[
            pl.BlockSpec(table.shape, lambda i: (0, 0, 0)),
            pl.BlockSpec((BAND_BINS, SIDE, 2 * SIDE), lambda i: (i, 0, 0)),
        ],
        out_specs=pl.BlockSpec((2, BAND_BINS, SIDE * SIDE), lambda i: (0, i, 0)),
        scratch_shapes=[pltpu.VMEM((BAND_BINS, 2 * SIDE, SIDE), jnp.float32)],
        compiler_params=pltpu.CompilerParams(vmem_limit_bytes=VMEM),
        name="finish",
    )(table, inner)


def compress_weights(replica, block_rows):
    taps = replica.shape[1]
    span = taps + block_rows

    def banded(vector):
        cycled = jnp.concatenate([vector, jnp.zeros((span + 1 - taps,), vector.dtype)])
        return jnp.tile(cycled, block_rows)[: block_rows * span].reshape(block_rows, span)

    real_rows = banded(replica[0])
    imag_rows = banded(replica[1])
    return jnp.stack(
        [
            jnp.concatenate([real_rows, -imag_rows], axis=0),
            jnp.concatenate([imag_rows, real_rows], axis=0),
        ]
    )


def per_device(echoes, replica, shifts, tap_counts, interp_weights, fm_rates):
    range_dev = echoes.shape[1]
    az_count = lax.axis_size("az")
    rg_count = lax.axis_size("rg")
    local_rows = range_dev // az_count
    block_rows = COMPRESS_ROWS
    bands_here = local_rows // BAND_BINS
    az_pos = lax.axis_index("az")
    rg_pos = lax.axis_index("rg")

    weights = compress_weights(replica, block_rows)
    forward_m, inverse_m, twist_cos, twist_sin = transform_tables()
    cosine = jnp.asarray(twist_cos, jnp.float32)
    sine = jnp.asarray(twist_sin, jnp.float32)
    forward_tables = (split_const(forward_m), cosine, sine)
    inverse_table = split_const(inverse_m)

    band_first = (rg_pos * range_dev + az_pos * local_rows) // BAND_BINS
    band_shift = lax.dynamic_slice_in_dim(shifts, band_first, bands_here)
    band_taps = lax.dynamic_slice_in_dim(tap_counts, band_first, bands_here)
    band_weight = lax.dynamic_slice_in_dim(interp_weights, band_first, bands_here)
    tap_index = lax.broadcasted_iota(jnp.int32, (bands_here, INTERP_TAPS), 1)
    live_weight = jnp.where(tap_index < band_taps[:, None], band_weight, 0.0)
    band_rate = lax.dynamic_slice_in_dim(fm_rates, band_first, bands_here)
    total_lines = SIDE * SIDE
    doppler = SIDE * lax.broadcasted_iota(jnp.int32, (SIDE, SIDE), 0) + lax.broadcasted_iota(
        jnp.int32, (SIDE, SIDE), 1
    )
    signed = (
        jnp.where(doppler < total_lines // 2, doppler, doppler - total_lines).astype(jnp.float32)
        / total_lines
    )
    phases = math.pi * band_rate[:, None, None] * (signed * signed)[None]
    pcos = jnp.cos(phases)
    psin = jnp.sin(phases)

    _, inner = exchange(
        band_shift, live_weight, weights, forward_tables, inverse_table, pcos, psin, echoes, az_count
    )
    return finish(inverse_table, inner)


def solution(mesh):
    return jax.shard_map(
        per_device,
        mesh=mesh,
        in_specs=(P(None, "rg", "az"), P(), P(), P(), P(), P()),
        out_specs=P(None, ("rg", "az"), None),
        check_vma=False,
    )
```

time: 647 us -> 537 us (0.83)
  Pallas kernels: 622 us -> 511 us
    pallas_call x2 -> x1, Pallas kernels: 196 us -> 32.4 us  [finish(): pl.pallas_call(finish_kernel, out_shape=jax.ShapeDtypeStruct((2, local_ro...]
    pallas_call x1, Pallas kernels: 425 us -> 479 us  [exchange(): pl.pallas_call(functools.partial(exchange_kernel, width, block_rows), out...]
where the time goes in v2:
time: 537 us; the launch traced here: 534 us
  Pallas kernels  511 us (95%)
  local copies, waits for them, and re-layouts  12.8 us (2%)
  other arithmetic  9.51 us (2%)
    pallas_call x1, Pallas kernels, exchange(): pl.pallas_call(functools.partial(exchange_kernel, width, block_rows), out...  479 us
    pallas_call x1, Pallas kernels, finish(): pl.pallas_call(finish_kernel, out_shape=jax.ShapeDtypeStruct((2, local_ro...  32.4 us

profile of v2, /device:TPU:29, one launch (start us, length us, event | category | flops | bytes accessed | tf_op | source)
XLA Modules:
  0.0 533.7 jit_solution(15260095552756059515)
XLA Ops:
  0.0 0.8 dynamic_slice.13
  0.8 0.8 dynamic-slice_multiply_fusion
  1.5 0.1 constant_dynamic-slice_fusion.1
  1.6 0.8 constant_dynamic-slice_fusion
  2.4 0.1 copy.18
  2.4 0.7 fusion.3.weight_ref
  3.1 0.7 copy.17.shift_ref
  3.8 0.8 slice_reduce_fusion
  4.6 0.1 fusion.2
  4.7 0.1 tile.8
  4.8 1.6 tile.9
  6.5 0.1 slice.16
  6.6 2.2 reshape.30
  8.7 0.1 tile.20
  8.8 1.6 tile.21
  10.5 1.1 slice.17
  11.6 2.8 reshape.31
  14.4 0.2 neg.3
  14.6 0.4 maximum_bitcast_fusion
  15.0 2.6 pad_maximum_fusion.w_ref
  17.6 4.8 multiply_sine_fusion
  22.4 478.9 %exchange.1 = (bf16[8,2,288,2048]{3,2,1,0:T(8,128)(2,1)}, bf16[256,128,256]{2,1,0:T(8,128)(2,1)}) custom-call(s32[16,8]{1,0:T(8,128)} %copy.17.shift_ref, f32[16,8]{1,0:T(8,128)} %fusion.3.weight_ref, bf16[2,512,2304]{2,1,0:T(8,128)(2,1)} %pad_maximum_fusion.w_ref, bf16[2,256,256]{2,1,0:T(8,128)(2,1)} %constant.79.ftable_ref, ...), custom_call_target="tpu_custom_call" | custom-call | flops 146028888064 | bytes 83886080 | tf_op jit(solution)/shard_map/exchange/pallas_call | solution.py:502
  501.3 0.0 copy-start.1
  501.3 32.4 %finish.1 = f32[2,256,16384]{2,1,0:T(8,128)} custom-call(bf16[2,256,256]{2,1,0:T(8,128)(2,1)} %constant.74.itable_ref.table_ref, bf16[256,128,256]{2,1,0:T(8,128)(2,1)} %get-tuple-element.6.inner_ref), custom_call_target="tpu_custom_call" | custom-call | tf_op jit(solution)/shard_map/finish/pallas_call | solution.py:560
  (8 shorter events, 0.0 us)
Async XLA Ops:
  0.0 1.5 copy-start
  11.6 3.0 copy-start.2
  501.3 32.4 %copy-start.1 = (s32[512,8]{0,1:T(8,128)S(1)}, s32[512,8]{0,1:T(8,128)}, u32[]{:S(2)}) copy-start(s32[512,8]{0,1:T(8,128)} %param.14) | copy-start | bytes 49156

commit v3 on v2

--- a/solution.py
+++ b/solution.py
@@ -61,15 +61,14 @@
 
 
 def phase_starts(bands):
-    cuts = [0, max(2, bands * 6 // 16), bands * 11 // 16, bands * 14 // 16]
-    return [at for k, at in enumerate(cuts) if k == 0 or at > cuts[k - 1]] + [bands]
+    return [0] + list(range(2, bands, 3)) + [bands]
 
 
 def exchange_kernel(
     width, block_rows,
-    shift_ref, weight_ref, w_ref, ftable_ref, itable_ref, cos_ref, sin_ref, pcos_ref, psin_ref,
+    shift_ref, weight_ref, rate_ref, replica_ref, ftable_ref, itable_ref, cos_ref, sin_ref,
     echoes_ref, turned_ref, inner_ref,
-    window, arrived, data, spectrum, moved, staged,
+    window, w_ref, arrived, data, spectrum, phase, staged,
     load_sem, rim_send, rim_recv, out_send, out_recv, halo_send, halo_recv, in_sem, inner_sem, token,
 ):
     az_count, rg_count = lax.axis_size("az"), lax.axis_size("rg")
@@ -189,6 +188,8 @@
 
             lax.fori_loop(0, az_count, clear_halo, 0)
 
+    fill_weights(replica_ref, w_ref)
+
     def rows_of(b, first, height):
         return pl.ds(pl.multiple_of(b * local_rows + first, BAND_BINS), height)
 
@@ -382,8 +383,8 @@
                 inner_store(band - 2).wait()
 
             migrate_band(
-                band, shift_ref, weight_ref, itable_ref, cos_ref, sin_ref, pcos_ref, psin_ref,
-                spectrum, moved, staged, lax.rem(band, 2),
+                band, shift_ref, weight_ref, rate_ref, itable_ref, cos_ref, sin_ref,
+                spectrum, data, phase, staged, lax.rem(band, 2),
             )
             inner_store(band).start()
 
@@ -421,39 +422,44 @@
                 rows, per, SIDE
             )
 
-    def pair(i, _):
-        both = jnp.concatenate([data[2 * i], data[2 * i + 1]], axis=1).astype(jnp.bfloat16)
-        first = mm2(table_ref, both, NN)
-        cosine, sine = cos_ref[...], sin_ref[...]
-        turned = []
-        for k in range(2):
-            real = first[:SIDE, k * SIDE : (k + 1) * SIDE]
-            imag = first[SIDE:, k * SIDE : (k + 1) * SIDE]
-            turned.append(
-                jnp.concatenate(
-                    [real * cosine + imag * sine, imag * cosine - real * sine], axis=1
-                )
-            )
-        second = mm3(table_ref, jnp.concatenate(turned, axis=0), NT)
-        for k in range(2):
-            spectrum[0, fresh + 2 * i + k] = second[:SIDE, k * SIDE : (k + 1) * SIDE]
-            spectrum[1, fresh + 2 * i + k] = second[SIDE:, k * SIDE : (k + 1) * SIDE]
-        return 0
-
-    lax.fori_loop(0, rows // 2, pair, 0, unroll=2)
+    both = jnp.concatenate([data[r].astype(jnp.bfloat16) for r in range(rows)], axis=1)
+    first = mm2(table_ref, both, NN)
+    cosine, sine = cos_ref[...], sin_ref[...]
+    turned = []
+    for r in range(rows):
+        real = first[:SIDE, r * SIDE : (r + 1) * SIDE]
+        imag = first[SIDE:, r * SIDE : (r + 1) * SIDE]
+        turned.append(
+            jnp.concatenate([real * cosine + imag * sine, imag * cosine - real * sine], axis=1)
+        )
+    second = mm3(table_ref, jnp.concatenate(turned, axis=0), NT)
+    for r in range(rows):
+        spectrum[0, fresh + r] = second[:SIDE, r * SIDE : (r + 1) * SIDE]
+        spectrum[1, fresh + r] = second[SIDE:, r * SIDE : (r + 1) * SIDE]
 
 
 def migrate_band(
-    band, shift_ref, weight_ref, table_ref, cos_ref, sin_ref, pcos_ref, psin_ref,
-    window, moved, staged, slot
+    band, shift_ref, weight_ref, rate_ref, table_ref, cos_ref, sin_ref,
+    window, moved, phase, staged, slot
 ):
     deep = SIDE // DOPPLER_BLOCKS
+    total_lines = SIDE * SIDE
+    doppler = SIDE * lax.broadcasted_iota(jnp.int32, (SIDE, SIDE), 0) + lax.broadcasted_iota(
+        jnp.int32, (SIDE, SIDE), 1
+    )
+    signed = (
+        jnp.where(doppler < total_lines // 2, doppler, doppler - total_lines).astype(jnp.float32)
+        / total_lines
+    )
+    angle = math.pi * rate_ref[band] * (signed * signed)
+    phase[0] = jnp.cos(angle)
+    phase[1] = jnp.sin(angle)
     taps = [weight_ref[band, t] for t in range(INTERP_TAPS)]
 
     def block(d, _):
         shift = shift_ref[band, d]
         spot = pl.ds(pl.multiple_of(d * deep, deep), deep)
-        pcos, psin = pcos_ref[band, spot, :], psin_ref[band, spot, :]
+        pcos, psin = phase[0, spot, :], phase[1, spot, :]
         for half in range(2):
             rows = BAND_BINS // 2
             parts = []
@@ -471,26 +477,22 @@
 
     lax.fori_loop(0, DOPPLER_BLOCKS, block, 0)
 
-    def pair(i, _):
-        both = jnp.concatenate([moved[2 * i], moved[2 * i + 1]], axis=1)
-        first = mm3(table_ref, both, NN)
-        cosine, sine = cos_ref[...], sin_ref[...]
-        for k in range(2):
-            real = first[:SIDE, k * SIDE : (k + 1) * SIDE]
-            imag = first[SIDE:, k * SIDE : (k + 1) * SIDE]
-            staged[slot, 2 * i + k, :, :SIDE] = (real * cosine - imag * sine).astype(jnp.bfloat16)
-            staged[slot, 2 * i + k, :, SIDE:] = (imag * cosine + real * sine).astype(jnp.bfloat16)
-        return 0
-
-    lax.fori_loop(0, BAND_BINS // 2, pair, 0, unroll=2)
-
-
-def exchange(shifts, live_weight, weights, ftables, itable, pcos, psin, echoes, az_count):
+    both = jnp.concatenate([moved[r] for r in range(BAND_BINS)], axis=1)
+    first = mm3(table_ref, both, NN)
+    cosine, sine = cos_ref[...], sin_ref[...]
+    for r in range(BAND_BINS):
+        real = first[:SIDE, r * SIDE : (r + 1) * SIDE]
+        imag = first[SIDE:, r * SIDE : (r + 1) * SIDE]
+        staged[slot, r, :, :SIDE] = (real * cosine - imag * sine).astype(jnp.bfloat16)
+        staged[slot, r, :, SIDE:] = (imag * cosine + real * sine).astype(jnp.bfloat16)
+
+
+def exchange(shifts, live_weight, rates, replica, ftables, itable, echoes, az_count):
     ftable, cosine, sine = ftables
     rows, lines = echoes.shape[1], echoes.shape[2]
-    span = weights.shape[2]
-    block_rows = weights.shape[1] // 2
-    taps = span - block_rows
+    taps = replica.shape[1]
+    block_rows = COMPRESS_ROWS
+    span = taps + block_rows
     width = math.gcd(256, lines)
     chunks = lines // width
     local_rows = rows // az_count
@@ -505,14 +507,15 @@
             jax.ShapeDtypeStruct((az_count, 2, local_rows + RIM_ROWS, lines), jnp.bfloat16),
             jax.ShapeDtypeStruct((local_rows, SIDE, 2 * SIDE), jnp.bfloat16),
         ],
-        in_specs=[smem, smem] + [vmem] * 7 + [anywhere],
+        in_specs=[smem] * 3 + [vmem] * 5 + [anywhere],
         out_specs=[anywhere, anywhere],
         scratch_shapes=[
             pltpu.VMEM((2, rows + taps, lines), jnp.bfloat16),
+            pltpu.VMEM((2, 2 * block_rows, span), jnp.bfloat16),
             pltpu.VMEM((2, az_count, 2, BAND_BINS, lines), jnp.bfloat16),
             pltpu.VMEM((BAND_BINS, 2 * SIDE, SIDE), jnp.float32),
             pltpu.VMEM((2, RIM_ROWS + BAND_BINS, SIDE, SIDE), jnp.float32),
-            pltpu.VMEM((BAND_BINS, 2 * SIDE, SIDE), jnp.float32),
+            pltpu.VMEM((2, SIDE, SIDE), jnp.float32),
             pltpu.VMEM((2, BAND_BINS, SIDE, 2 * SIDE), jnp.bfloat16),
             dma((chunks,)),
             dma((chunks,)),
@@ -534,18 +537,14 @@
             transcendentals=0,
         ),
         name="exchange",
-    )(shifts, live_weight, weights, ftable, itable, cosine, sine, pcos, psin, echoes)
+    )(shifts, live_weight, rates, replica, ftable, itable, cosine, sine, echoes)
 
 
 def finish_kernel(table_ref, inner_ref, out_ref, image):
-    def pair(i, _):
-        both = jnp.concatenate([inner_ref[2 * i], inner_ref[2 * i + 1]], axis=0)
-        second = mm2(table_ref, both, NT) * (1.0 / (SIDE * SIDE))
-        for k in range(2):
-            image[2 * i + k] = second[:, k * SIDE : (k + 1) * SIDE]
-        return 0
-
-    lax.fori_loop(0, BAND_BINS // 2, pair, 0, unroll=2)
+    both = jnp.concatenate([inner_ref[r] for r in range(BAND_BINS)], axis=0)
+    second = mm2(table_ref, both, NT) * (1.0 / (SIDE * SIDE))
+    for r in range(BAND_BINS):
+        image[r] = second[:, r * SIDE : (r + 1) * SIDE]
     group = 16
     for c in range(2):
         for g in range(SIDE // group):
@@ -572,22 +571,22 @@
     )(table, inner)
 
 
-def compress_weights(replica, block_rows):
-    taps = replica.shape[1]
-    span = taps + block_rows
-
-    def banded(vector):
-        cycled = jnp.concatenate([vector, jnp.zeros((span + 1 - taps,), vector.dtype)])
-        return jnp.tile(cycled, block_rows)[: block_rows * span].reshape(block_rows, span)
-
-    real_rows = banded(replica[0])
-    imag_rows = banded(replica[1])
-    return jnp.stack(
-        [
-            jnp.concatenate([real_rows, -imag_rows], axis=0),
-            jnp.concatenate([imag_rows, real_rows], axis=0),
-        ]
-    )
+def fill_weights(replica_ref, w_ref):
+    count, span = w_ref.shape[1] // 2, w_ref.shape[2]
+    taps = replica_ref[...].astype(jnp.float32)
+    for c in range(2):
+        padded = jnp.concatenate(
+            [taps[c : c + 1], jnp.zeros((1, span - taps.shape[1]), jnp.float32)], axis=1
+        )
+        rows = pltpu.roll(
+            jnp.broadcast_to(padded, (count, span)), 0, 1, stride=1, stride_axis=0
+        )
+        if c == 0:
+            w_ref[0, :count] = rows.astype(jnp.bfloat16)
+            w_ref[1, count:] = rows.astype(jnp.bfloat16)
+        else:
+            w_ref[0, count:] = (-rows).astype(jnp.bfloat16)
+            w_ref[1, :count] = rows.astype(jnp.bfloat16)
 
 
 def per_device(echoes, replica, shifts, tap_counts, interp_weights, fm_rates):
@@ -595,12 +594,10 @@
     az_count = lax.axis_size("az")
     rg_count = lax.axis_size("rg")
     local_rows = range_dev // az_count
-    block_rows = COMPRESS_ROWS
     bands_here = local_rows // BAND_BINS
     az_pos = lax.axis_index("az")
     rg_pos = lax.axis_index("rg")
 
-    weights = compress_weights(replica, block_rows)
     forward_m, inverse_m, twist_cos, twist_sin = transform_tables()
     cosine = jnp.asarray(twist_cos, jnp.float32)
     sine = jnp.asarray(twist_sin, jnp.float32)
@@ -614,20 +611,8 @@
     tap_index = lax.broadcasted_iota(jnp.int32, (bands_here, INTERP_TAPS), 1)
     live_weight = jnp.where(tap_index < band_taps[:, None], band_weight, 0.0)
     band_rate = lax.dynamic_slice_in_dim(fm_rates, band_first, bands_here)
-    total_lines = SIDE * SIDE
-    doppler = SIDE * lax.broadcasted_iota(jnp.int32, (SIDE, SIDE), 0) + lax.broadcasted_iota(
-        jnp.int32, (SIDE, SIDE), 1
-    )
-    signed = (
-        jnp.where(doppler < total_lines // 2, doppler, doppler - total_lines).astype(jnp.float32)
-        / total_lines
-    )
-    phases = math.pi * band_rate[:, None, None] * (signed * signed)[None]
-    pcos = jnp.cos(phases)
-    psin = jnp.sin(phases)
-
     _, inner = exchange(
-        band_shift, live_weight, weights, forward_tables, inverse_table, pcos, psin, echoes, az_count
+        band_shift, live_weight, band_rate, replica, forward_tables, inverse_table, echoes, az_count
     )
     return finish(inverse_table, inner)
 

time: 537 us -> 462 us (0.86)
  Pallas kernels: 511 us -> 456 us
  local copies, waits for them, and re-layouts: 12.8 us -> 3.69 us
  other arithmetic: 9.51 us -> 0.67 us
    pallas_call x1, Pallas kernels: 479 us -> 431 us  [exchange(): pl.pallas_call(functools.partial(exchange_kernel, width, block_rows), out...]
    pallas_call x1, Pallas kernels: 32.4 us -> 25.4 us  [finish(): pl.pallas_call(finish_kernel, out_shape=jax.ShapeDtypeStruct((2, local_ro...]
where the time goes in v3:
time: 462 us; the launch traced here: 461 us
  Pallas kernels  456 us (99%)
    pallas_call x1, Pallas kernels, exchange(): pl.pallas_call(functools.partial(exchange_kernel, width, block_rows), out...  431 us
    pallas_call x1, Pallas kernels, finish(): pl.pallas_call(finish_kernel, out_shape=jax.ShapeDtypeStruct((2, local_ro...  25.4 us

profile of v3, /device:TPU:29, one launch (start us, length us, event | category | flops | bytes accessed | tf_op | source)
XLA Modules:
  0.0 460.6 jit_solution(15947823417277412555)
XLA Ops:
  0.0 0.0 copy-start
  0.0 0.8 dynamic_slice.13
  0.8 1.3 dynamic_slice.15.rate_ref
  2.1 0.0 copy-done
  2.1 0.1 constant_dynamic-slice_fusion.1
  2.2 0.8 constant_dynamic-slice_fusion
  2.9 0.1 copy.16
  3.0 0.7 fusion.weight_ref
  3.7 0.7 copy.15.shift_ref
  4.4 430.8 %exchange.1 = (bf16[8,2,288,2048]{3,2,1,0:T(8,128)(2,1)}, bf16[256,128,256]{2,1,0:T(8,128)(2,1)}) custom-call(s32[16,8]{1,0:T(8,128)} %copy.15.shift_ref, f32[16,8]{1,0:T(8,128)} %fusion.weight_ref, f32[16]{0:T(128)} %dynamic_slice.15.rate_ref, bf16[2,2048]{1,0:T(2,128)(2,1)} %replica_ref.1, bf16[2,256,256]{2,1,0:T(8,128)(2,1)} %constant.61.ftable_ref, ...), custom_call_target="tpu_custom_call" | custom-call | flops 146028888064 | bytes 83886080 | tf_op jit(solution)/shard_map/exchange/pallas_call | solution.py:504
  435.2 0.0 copy-start.1
  435.2 25.4 %finish.1 = f32[2,256,16384]{2,1,0:T(8,128)} custom-call(bf16[2,256,256]{2,1,0:T(8,128)(2,1)} %constant.56.itable_ref.table_ref, bf16[256,128,256]{2,1,0:T(8,128)(2,1)} %get-tuple-element.6.inner_ref), custom_call_target="tpu_custom_call" | custom-call | tf_op jit(solution)/shard_map/finish/pallas_call | solution.py:559
  460.6 0.0 copy-done.1
Async XLA Ops:
  0.0 2.1 copy-start
  435.2 25.4 %copy-start.1 = (s32[512,8]{0,1:T(8,128)S(1)}, s32[512,8]{0,1:T(8,128)}, u32[]{:S(2)}) copy-start(s32[512,8]{0,1:T(8,128)} %param.14) | copy-start | bytes 49156

commit v4 on v3

--- a/solution.py
+++ b/solution.py
@@ -61,12 +61,12 @@
 
 
 def phase_starts(bands):
-    return [0] + list(range(2, bands, 3)) + [bands]
+    return [0] + list(range(2, bands - 1, 3)) + [bands - 1, bands]
 
 
 def exchange_kernel(
     width, block_rows,
-    shift_ref, weight_ref, rate_ref, replica_ref, ftable_ref, itable_ref, cos_ref, sin_ref,
+    shift_ref, count_ref, weight_ref, rate_ref, replica_ref, ftable_ref, itable_ref, cos_ref, sin_ref,
     echoes_ref, turned_ref, inner_ref,
     window, w_ref, arrived, data, spectrum, phase, staged,
     load_sem, rim_send, rim_recv, out_send, out_recv, halo_send, halo_recv, in_sem, inner_sem, token,
@@ -157,7 +157,12 @@
         + last * one(has_after & (a == last)),
     )
 
-    upfront = jnp.where(late, chunks, min(2, chunks))
+    def rim_sent(c):
+        rim_copy(c).wait_send()
+
+        @pl.when(c + 2 < chunks)
+        def _():
+            rim_copy(c + 2).start()
 
     @pl.when(has_before)
     def _():
@@ -165,7 +170,17 @@
             rim_copy(c).start()
             return 0
 
-        lax.fori_loop(0, upfront, start_rim, 0)
+        lax.fori_loop(0, min(2, chunks), start_rim, 0)
+
+    fill_weights(replica_ref, w_ref)
+
+    @pl.when(late)
+    def _():
+        def next_rim(c, _):
+            rim_sent(c)
+            return 0
+
+        lax.fori_loop(0, chunks, next_rim, 0)
 
     @pl.when(jnp.logical_not(has_after))
     def _():
@@ -187,8 +202,6 @@
                 return 0
 
             lax.fori_loop(0, az_count, clear_halo, 0)
-
-    fill_weights(replica_ref, w_ref)
 
     def rows_of(b, first, height):
         return pl.ds(pl.multiple_of(b * local_rows + first, BAND_BINS), height)
@@ -264,13 +277,9 @@
         def _():
             send_blocks(0, local_rows, cols, c, 0)
 
-        @pl.when(has_before)
-        def _():
-            rim_copy(c).wait_send()
-
-            @pl.when(c + upfront < chunks)
-            def _():
-                rim_copy(c + upfront).start()
+        @pl.when(has_before & early)
+        def _():
+            rim_sent(c)
 
         return 0
 
@@ -327,15 +336,14 @@
             landed = turned_ref.at[:, :, pl.ds(starts[p] * BAND_BINS, height_of(p)), :]
             pltpu.make_async_copy(landed, landed, out_recv.at[p]).wait()
 
-    total_bands = bands + RIM_ROWS // BAND_BINS
+    halo_bands = RIM_ROWS // BAND_BINS
     fresh = RIM_ROWS
 
     def band_load(i):
-        slot = lax.rem(i, 2)
         return pltpu.make_async_copy(
             turned_ref.at[:, :, pl.ds(pl.multiple_of(i * BAND_BINS, BAND_BINS), BAND_BINS), :],
-            arrived.at[slot],
-            in_sem.at[slot],
+            arrived,
+            in_sem.at[0],
         )
 
     def inner_store(band):
@@ -346,56 +354,67 @@
             inner_sem.at[slot],
         )
 
+    halo_step = starts[max(phases - 2, 0)]
+    band_first = (g * rows + a * local_rows) // BAND_BINS
+
     def band_step(i, _):
-        for p in range(phases):
-            @pl.when(i == starts[p])
+        @pl.when(i == 0)
+        def _():
+            enter_phase(0)
+
+            @pl.when(passes_halo)
             def _():
-                enter_phase(p)
-                if p == 0:
-                    @pl.when(passes_halo)
-                    def _():
-                        neighbour_halo.start()
-                band_load(i).start()
-
-        @pl.when(i == bands)
+                neighbour_halo.start()
+
+        @pl.when(i == halo_step)
         def _():
             whole_halo = turned_ref.at[:, :, halo_rows, :]
             pltpu.make_async_copy(whole_halo, whole_halo, halo_recv.at[0]).wait()
-            band_load(i).start()
-
-        band_load(i).wait()
-        opens = i + 1 == total_bands
-        for at in starts:
-            opens = opens | (i + 1 == at)
-
-        @pl.when(jnp.logical_not(opens))
-        def _():
-            band_load(i + 1).start()
-
-        forward_band(lax.rem(i, 2), ftable_ref, cos_ref, sin_ref, arrived, data, spectrum, fresh)
-
-        @pl.when(i >= 2)
-        def _():
-            band = i - 2
-
+
+        def transform(k, _):
+            is_own = k == halo_bands
+            for p in range(1, phases):
+                @pl.when(is_own & (i == starts[p]))
+                def _():
+                    enter_phase(p)
+
+            load = band_load(jnp.where(is_own, i, bands + k))
+            load.start()
+            load.wait()
+            forward_band(
+                ftable_ref, cos_ref, sin_ref, arrived, data, spectrum,
+                jnp.where(is_own, fresh, fresh + BAND_BINS * (k + 1)),
+            )
+            return 0
+
+        lax.fori_loop(
+            jnp.where(i == halo_step, 0, halo_bands), halo_bands + 1, transform, 0
+        )
+
+        def migrate(band, _):
             @pl.when(band >= 2)
             def _():
                 inner_store(band - 2).wait()
 
             migrate_band(
-                band, shift_ref, weight_ref, rate_ref, itable_ref, cos_ref, sin_ref,
-                spectrum, data, phase, staged, lax.rem(band, 2),
+                band_first + band, (band - i + 2) * BAND_BINS, shift_ref, count_ref, weight_ref,
+                rate_ref, itable_ref,
+                cos_ref, sin_ref, spectrum, data, phase, staged, lax.rem(band, 2),
             )
             inner_store(band).start()
+            return 0
+
+        is_last = i == bands - 1
+        lax.fori_loop(jnp.maximum(i - 2, 0), jnp.where(is_last, bands, i - 1), migrate, 0)
 
         def slide(r, _):
             spectrum[:, r] = spectrum[:, r + BAND_BINS]
             return 0
 
-        lax.fori_loop(0, fresh, slide, 0)
+        lax.fori_loop(0, jnp.where(is_last, 0, fresh), slide, 0)
         return 0
 
-    lax.fori_loop(0, total_bands, band_step, 0)
+    lax.fori_loop(0, bands, band_step, 0)
     for band in range(max(0, bands - 2), bands):
         inner_store(band).wait()
 
@@ -412,12 +431,12 @@
         neighbour_halo.wait_send()
 
 
-def forward_band(slot, table_ref, cos_ref, sin_ref, arrived, data, spectrum, fresh):
-    _, az_count, _, rows, lines = arrived.shape
+def forward_band(table_ref, cos_ref, sin_ref, arrived, data, spectrum, fresh):
+    az_count, _, rows, lines = arrived.shape
     per = lines // SIDE
     for source in range(az_count):
         for c in range(2):
-            piece = arrived[slot, source, c].astype(jnp.float32)
+            piece = arrived[source, c].astype(jnp.float32)
             data[:, c * SIDE + source * per : c * SIDE + (source + 1) * per, :] = piece.reshape(
                 rows, per, SIDE
             )
@@ -439,7 +458,7 @@
 
 
 def migrate_band(
-    band, shift_ref, weight_ref, rate_ref, table_ref, cos_ref, sin_ref,
+    place, base, shift_ref, count_ref, weight_ref, rate_ref, table_ref, cos_ref, sin_ref,
     window, moved, phase, staged, slot
 ):
     deep = SIDE // DOPPLER_BLOCKS
@@ -451,13 +470,15 @@
         jnp.where(doppler < total_lines // 2, doppler, doppler - total_lines).astype(jnp.float32)
         / total_lines
     )
-    angle = math.pi * rate_ref[band] * (signed * signed)
+    angle = math.pi * rate_ref[place] * (signed * signed)
     phase[0] = jnp.cos(angle)
     phase[1] = jnp.sin(angle)
-    taps = [weight_ref[band, t] for t in range(INTERP_TAPS)]
+    taps = [
+        jnp.where(t < count_ref[place], weight_ref[t, place], 0.0) for t in range(INTERP_TAPS)
+    ]
 
     def block(d, _):
-        shift = shift_ref[band, d]
+        shift = base + shift_ref[d, place]
         spot = pl.ds(pl.multiple_of(d * deep, deep), deep)
         pcos, psin = phase[0, spot, :], phase[1, spot, :]
         for half in range(2):
@@ -487,7 +508,7 @@
         staged[slot, r, :, SIDE:] = (imag * cosine + real * sine).astype(jnp.bfloat16)
 
 
-def exchange(shifts, live_weight, rates, replica, ftables, itable, echoes, az_count):
+def exchange(shifts, counts, factors, rates, replica, ftables, itable, echoes, az_count):
     ftable, cosine, sine = ftables
     rows, lines = echoes.shape[1], echoes.shape[2]
     taps = replica.shape[1]
@@ -507,14 +528,14 @@
             jax.ShapeDtypeStruct((az_count, 2, local_rows + RIM_ROWS, lines), jnp.bfloat16),
             jax.ShapeDtypeStruct((local_rows, SIDE, 2 * SIDE), jnp.bfloat16),
         ],
-        in_specs=[smem] * 3 + [vmem] * 5 + [anywhere],
+        in_specs=[smem] * 4 + [vmem] * 5 + [anywhere],
         out_specs=[anywhere, anywhere],
         scratch_shapes=[
             pltpu.VMEM((2, rows + taps, lines), jnp.bfloat16),
             pltpu.VMEM((2, 2 * block_rows, span), jnp.bfloat16),
-            pltpu.VMEM((2, az_count, 2, BAND_BINS, lines), jnp.bfloat16),
+            pltpu.VMEM((az_count, 2, BAND_BINS, lines), jnp.bfloat16),
             pltpu.VMEM((BAND_BINS, 2 * SIDE, SIDE), jnp.float32),
-            pltpu.VMEM((2, RIM_ROWS + BAND_BINS, SIDE, SIDE), jnp.float32),
+            pltpu.VMEM((2, 2 * RIM_ROWS + BAND_BINS, SIDE, SIDE), jnp.float32),
             pltpu.VMEM((2, SIDE, SIDE), jnp.float32),
             pltpu.VMEM((2, BAND_BINS, SIDE, 2 * SIDE), jnp.bfloat16),
             dma((chunks,)),
@@ -524,7 +545,7 @@
             dma((phases,)),
             dma((3,)),
             dma((1,)),
-            dma((2,)),
+            dma((1,)),
             dma((2,)),
             pltpu.SemaphoreType.REGULAR,
         ],
@@ -537,35 +558,37 @@
             transcendentals=0,
         ),
         name="exchange",
-    )(shifts, live_weight, rates, replica, ftable, itable, cosine, sine, echoes)
+    )(shifts.T, counts, factors.T, rates, replica, ftable, itable, cosine, sine, echoes)
 
 
 def finish_kernel(table_ref, inner_ref, out_ref, image):
-    both = jnp.concatenate([inner_ref[r] for r in range(BAND_BINS)], axis=0)
+    rows = inner_ref.shape[0]
+    both = jnp.concatenate([inner_ref[r] for r in range(rows)], axis=0)
     second = mm2(table_ref, both, NT) * (1.0 / (SIDE * SIDE))
-    for r in range(BAND_BINS):
+    for r in range(rows):
         image[r] = second[:, r * SIDE : (r + 1) * SIDE]
     group = 16
     for c in range(2):
         for g in range(SIDE // group):
             piece = image[:, c * SIDE + g * group : c * SIDE + (g + 1) * group, :]
             out_ref[c, :, g * group * SIDE : (g + 1) * group * SIDE] = piece.reshape(
-                BAND_BINS, group * SIDE
+                rows, group * SIDE
             )
 
 
 def finish(table, inner):
     local_rows = inner.shape[0]
+    rows = math.gcd(32, local_rows)
     return pl.pallas_call(
         finish_kernel,
         out_shape=jax.ShapeDtypeStruct((2, local_rows, SIDE * SIDE), jnp.float32),
-        grid=(local_rows // BAND_BINS,),
+        grid=(local_rows // rows,),
         in_specs=[
             pl.BlockSpec(table.shape, lambda i: (0, 0, 0)),
-            pl.BlockSpec((BAND_BINS, SIDE, 2 * SIDE), lambda i: (i, 0, 0)),
+            pl.BlockSpec((rows, SIDE, 2 * SIDE), lambda i: (i, 0, 0)),
         ],
-        out_specs=pl.BlockSpec((2, BAND_BINS, SIDE * SIDE), lambda i: (0, i, 0)),
-        scratch_shapes=[pltpu.VMEM((BAND_BINS, 2 * SIDE, SIDE), jnp.float32)],
+        out_specs=pl.BlockSpec((2, rows, SIDE * SIDE), lambda i: (0, i, 0)),
+        scratch_shapes=[pltpu.VMEM((rows, 2 * SIDE, SIDE), jnp.float32)],
         compiler_params=pltpu.CompilerParams(vmem_limit_bytes=VMEM),
         name="finish",
     )(table, inner)
@@ -590,29 +613,15 @@
 
 
 def per_device(echoes, replica, shifts, tap_counts, interp_weights, fm_rates):
-    range_dev = echoes.shape[1]
     az_count = lax.axis_size("az")
-    rg_count = lax.axis_size("rg")
-    local_rows = range_dev // az_count
-    bands_here = local_rows // BAND_BINS
-    az_pos = lax.axis_index("az")
-    rg_pos = lax.axis_index("rg")
-
     forward_m, inverse_m, twist_cos, twist_sin = transform_tables()
     cosine = jnp.asarray(twist_cos, jnp.float32)
     sine = jnp.asarray(twist_sin, jnp.float32)
     forward_tables = (split_const(forward_m), cosine, sine)
     inverse_table = split_const(inverse_m)
 
-    band_first = (rg_pos * range_dev + az_pos * local_rows) // BAND_BINS
-    band_shift = lax.dynamic_slice_in_dim(shifts, band_first, bands_here)
-    band_taps = lax.dynamic_slice_in_dim(tap_counts, band_first, bands_here)
-    band_weight = lax.dynamic_slice_in_dim(interp_weights, band_first, bands_here)
-    tap_index = lax.broadcasted_iota(jnp.int32, (bands_here, INTERP_TAPS), 1)
-    live_weight = jnp.where(tap_index < band_taps[:, None], band_weight, 0.0)
-    band_rate = lax.dynamic_slice_in_dim(fm_rates, band_first, bands_here)
     _, inner = exchange(
-        band_shift, live_weight, band_rate, replica, forward_tables, inverse_table, echoes, az_count
+        shifts, tap_counts, interp_weights, fm_rates, replica, forward_tables, inverse_table, echoes, az_count
     )
     return finish(inverse_table, inner)
 

time: 462 us -> 461 us (level)
  no operation moved by 1% of the time
where the time goes in v4:
time: 461 us; the launch traced here: 456 us
  Pallas kernels  456 us (99%)
    pallas_call x1, Pallas kernels, exchange(): pl.pallas_call(functools.partial(exchange_kernel, width, block_rows), out...  434 us
    pallas_call x1, Pallas kernels, finish(): pl.pallas_call(finish_kernel, out_shape=jax.ShapeDtypeStruct((2, local_ro...  22.5 us

profile of v4, /device:TPU:29, one launch (start us, length us, event | category | flops | bytes accessed | tf_op | source)
XLA Modules:
  0.0 456.4 jit_solution(12462957855509528813)
XLA Ops:
  0.0 433.9 %exchange.1 = (bf16[8,2,288,2048]{3,2,1,0:T(8,128)(2,1)}, bf16[256,128,256]{2,1,0:T(8,128)(2,1)}) custom-call(s32[8,512]{1,0:T(8,128)} %bitcast.2, s32[512]{0:T(512)} %count_ref.1, f32[8,512]{1,0:T(8,128)} %bitcast.3, f32[512]{0:T(512)} %rate_ref.1, bf16[2,2048]{1,0:T(2,128)(2,1)} %replica_ref.1, bf16[2,256,256]{2,1,0:T(8,128)(2,1)} %constant.27.ftable_ref, ...), custom_call_target="tpu_custom_call" | custom-call | flops 146028888064 | bytes 83886080 | tf_op jit(solution)/shard_map/exchange/pallas_call | solution.py:525
  433.9 22.5 %finish.1 = f32[2,256,16384]{2,1,0:T(8,128)} custom-call(bf16[2,256,256]{2,1,0:T(8,128)(2,1)} %constant.22.itable_ref.table_ref, bf16[256,128,256]{2,1,0:T(8,128)(2,1)} %get-tuple-element.6.inner_ref), custom_call_target="tpu_custom_call" | custom-call | tf_op jit(solution)/shard_map/finish/pallas_call | solution.py:582

commit v5 on v4

--- a/solution.py
+++ b/solution.py
@@ -61,7 +61,7 @@
 
 
 def phase_starts(bands):
-    return [0] + list(range(2, bands - 1, 3)) + [bands - 1, bands]
+    return list(range(0, bands, 2)) + [bands]
 
 
 def exchange_kernel(
@@ -323,27 +323,26 @@
     @pl.when(late)
     def _():
         pl.semaphore_wait(token, 1)
-        send_phase(0)
-        if phases > 1:
-            send_phase(1)
+        for p in range(0, min(4, phases)):
+            send_phase(p)
 
     def enter_phase(p):
         @pl.when(late)
         def _():
             sent_blocks(height_of(p), whole_lines, p)
-            if p + 2 < phases:
-                send_phase(p + 2)
+            if p + 4 < phases:
+                send_phase(p + 4)
             landed = turned_ref.at[:, :, pl.ds(starts[p] * BAND_BINS, height_of(p)), :]
             pltpu.make_async_copy(landed, landed, out_recv.at[p]).wait()
 
     halo_bands = RIM_ROWS // BAND_BINS
     fresh = RIM_ROWS
 
-    def band_load(i):
+    def band_load(i, slot):
         return pltpu.make_async_copy(
             turned_ref.at[:, :, pl.ds(pl.multiple_of(i * BAND_BINS, BAND_BINS), BAND_BINS), :],
-            arrived,
-            in_sem.at[0],
+            arrived.at[slot],
+            in_sem.at[slot],
         )
 
     def inner_store(band):
@@ -357,39 +356,52 @@
     halo_step = starts[max(phases - 2, 0)]
     band_first = (g * rows + a * local_rows) // BAND_BINS
 
+    enter_phase(0)
+
+    @pl.when(passes_halo)
+    def _():
+        neighbour_halo.start()
+
+    band_load(0, 0).start()
+
     def band_step(i, _):
-        @pl.when(i == 0)
-        def _():
-            enter_phase(0)
-
-            @pl.when(passes_halo)
-            def _():
-                neighbour_halo.start()
-
         @pl.when(i == halo_step)
         def _():
             whole_halo = turned_ref.at[:, :, halo_rows, :]
             pltpu.make_async_copy(whole_halo, whole_halo, halo_recv.at[0]).wait()
 
+        is_last = i == bands - 1
+        turn = jnp.where(i < halo_step, lax.rem(i, 3), 0)
+        row = fresh + BAND_BINS * turn
+
         def transform(k, _):
             is_own = k == halo_bands
-            for p in range(1, phases):
-                @pl.when(is_own & (i == starts[p]))
-                def _():
-                    enter_phase(p)
-
-            load = band_load(jnp.where(is_own, i, bands + k))
-            load.start()
+            slot = lax.rem(jnp.where(is_own, i, i + 1), 2)
+            load = band_load(jnp.where(is_own, i, bands + k), slot)
+
+            @pl.when(jnp.logical_not(is_own))
+            def _():
+                load.start()
+
             load.wait()
             forward_band(
-                ftable_ref, cos_ref, sin_ref, arrived, data, spectrum,
-                jnp.where(is_own, fresh, fresh + BAND_BINS * (k + 1)),
+                slot, ftable_ref, cos_ref, sin_ref, arrived, data, spectrum,
+                jnp.where(is_own, row, fresh + BAND_BINS * (k + 1)),
             )
             return 0
 
         lax.fori_loop(
             jnp.where(i == halo_step, 0, halo_bands), halo_bands + 1, transform, 0
         )
+
+        for p in range(1, phases):
+            @pl.when(i + 1 == starts[p])
+            def _():
+                enter_phase(p)
+
+        @pl.when(jnp.logical_not(is_last))
+        def _():
+            band_load(i + 1, lax.rem(i + 1, 2)).start()
 
         def migrate(band, _):
             @pl.when(band >= 2)
@@ -397,21 +409,21 @@
                 inner_store(band - 2).wait()
 
             migrate_band(
-                band_first + band, (band - i + 2) * BAND_BINS, shift_ref, count_ref, weight_ref,
+                band_first + band, row - fresh + (band - i + 2) * BAND_BINS, shift_ref, count_ref, weight_ref,
                 rate_ref, itable_ref,
                 cos_ref, sin_ref, spectrum, data, phase, staged, lax.rem(band, 2),
             )
             inner_store(band).start()
             return 0
 
-        is_last = i == bands - 1
         lax.fori_loop(jnp.maximum(i - 2, 0), jnp.where(is_last, bands, i - 1), migrate, 0)
 
         def slide(r, _):
-            spectrum[:, r] = spectrum[:, r + BAND_BINS]
-            return 0
-
-        lax.fori_loop(0, jnp.where(is_last, 0, fresh), slide, 0)
+            spectrum[:, r] = spectrum[:, r + BAND_BINS * (turn + 1)]
+            return 0
+
+        full = (turn == 2) | (i >= halo_step - 1)
+        lax.fori_loop(0, jnp.where(full & jnp.logical_not(is_last), fresh, 0), slide, 0)
         return 0
 
     lax.fori_loop(0, bands, band_step, 0)
@@ -431,12 +443,12 @@
         neighbour_halo.wait_send()
 
 
-def forward_band(table_ref, cos_ref, sin_ref, arrived, data, spectrum, fresh):
-    az_count, _, rows, lines = arrived.shape
+def forward_band(slot, table_ref, cos_ref, sin_ref, arrived, data, spectrum, fresh):
+    _, az_count, _, rows, lines = arrived.shape
     per = lines // SIDE
     for source in range(az_count):
         for c in range(2):
-            piece = arrived[source, c].astype(jnp.float32)
+            piece = arrived[slot, source, c].astype(jnp.float32)
             data[:, c * SIDE + source * per : c * SIDE + (source + 1) * per, :] = piece.reshape(
                 rows, per, SIDE
             )
@@ -533,7 +545,7 @@
         scratch_shapes=[
             pltpu.VMEM((2, rows + taps, lines), jnp.bfloat16),
             pltpu.VMEM((2, 2 * block_rows, span), jnp.bfloat16),
-            pltpu.VMEM((az_count, 2, BAND_BINS, lines), jnp.bfloat16),
+            pltpu.VMEM((2, az_count, 2, BAND_BINS, lines), jnp.bfloat16),
             pltpu.VMEM((BAND_BINS, 2 * SIDE, SIDE), jnp.float32),
             pltpu.VMEM((2, 2 * RIM_ROWS + BAND_BINS, SIDE, SIDE), jnp.float32),
             pltpu.VMEM((2, SIDE, SIDE), jnp.float32),
@@ -545,7 +557,7 @@
             dma((phases,)),
             dma((3,)),
             dma((1,)),
-            dma((1,)),
+            dma((2,)),
             dma((2,)),
             pltpu.SemaphoreType.REGULAR,
         ],

time: 461 us -> 447 us (0.970)
  Pallas kernels: 456 us -> 444 us
    pallas_call x1, Pallas kernels: 434 us -> 422 us  [exchange(): pl.pallas_call(functools.partial(exchange_kernel, width, block_rows), out...]
where the time goes in v5:
time: 447 us; the launch traced here: 444 us
  Pallas kernels  444 us (99%)
    pallas_call x1, Pallas kernels, exchange(): pl.pallas_call(functools.partial(exchange_kernel, width, block_rows), out...  422 us
    pallas_call x1, Pallas kernels, finish(): pl.pallas_call(finish_kernel, out_shape=jax.ShapeDtypeStruct((2, local_ro...  22.5 us

profile of v5, /device:TPU:29, one launch (start us, length us, event | category | flops | bytes accessed | tf_op | source)
XLA Modules:
  0.0 444.3 jit_solution(5539641146501002903)
XLA Ops:
  0.0 421.9 %exchange.1 = (bf16[8,2,288,2048]{3,2,1,0:T(8,128)(2,1)}, bf16[256,128,256]{2,1,0:T(8,128)(2,1)}) custom-call(s32[8,512]{1,0:T(8,128)} %bitcast.2, s32[512]{0:T(512)} %count_ref.1, f32[8,512]{1,0:T(8,128)} %bitcast.3, f32[512]{0:T(512)} %rate_ref.1, bf16[2,2048]{1,0:T(2,128)(2,1)} %replica_ref.1, bf16[2,256,256]{2,1,0:T(8,128)(2,1)} %constant.27.ftable_ref, ...), custom_call_target="tpu_custom_call" | custom-call | flops 146028888064 | bytes 83886080 | tf_op jit(solution)/shard_map/exchange/pallas_call | solution.py:537
  421.9 22.5 %finish.1 = f32[2,256,16384]{2,1,0:T(8,128)} custom-call(bf16[2,256,256]{2,1,0:T(8,128)(2,1)} %constant.22.itable_ref.table_ref, bf16[256,128,256]{2,1,0:T(8,128)(2,1)} %get-tuple-element.6.inner_ref), custom_call_target="tpu_custom_call" | custom-call | tf_op jit(solution)/shard_map/finish/pallas_call | solution.py:594

commit v6 on v5

--- a/solution.py
+++ b/solution.py
@@ -61,14 +61,14 @@
 
 
 def phase_starts(bands):
-    return list(range(0, bands, 2)) + [bands]
+    return list(range(0, bands - 1, 2)) + [bands - 1, bands]
 
 
 def exchange_kernel(
     width, block_rows,
     shift_ref, count_ref, weight_ref, rate_ref, replica_ref, ftable_ref, itable_ref, cos_ref, sin_ref,
     echoes_ref, turned_ref, inner_ref,
-    window, w_ref, arrived, data, spectrum, phase, staged,
+    window, ahead, w_ref, arrived, data, spectrum, phase, staged,
     load_sem, rim_send, rim_recv, out_send, out_recv, halo_send, halo_recv, in_sem, inner_sem, token,
 ):
     az_count, rg_count = lax.axis_size("az"), lax.axis_size("rg")
@@ -157,12 +157,14 @@
         + last * one(has_after & (a == last)),
     )
 
+    flying = jnp.where(late, min(2, chunks), min(4, chunks))
+
     def rim_sent(c):
         rim_copy(c).wait_send()
 
-        @pl.when(c + 2 < chunks)
-        def _():
-            rim_copy(c + 2).start()
+        @pl.when(c + flying < chunks)
+        def _():
+            rim_copy(c + flying).start()
 
     @pl.when(has_before)
     def _():
@@ -170,7 +172,7 @@
             rim_copy(c).start()
             return 0
 
-        lax.fori_loop(0, min(2, chunks), start_rim, 0)
+        lax.fori_loop(0, flying, start_rim, 0)
 
     fill_weights(replica_ref, w_ref)
 
@@ -254,6 +256,40 @@
     )
     passes_halo = (a > 0) & (a != middle + 1)
 
+    half_rows = rows // 2
+    half_blocks = half_rows // block_rows
+
+    def send_half(source, skipped, first_dest, cols, c):
+        here = cols if source is window else pl.ds(0, width)
+
+        def one_block(d, _):
+            b = first_dest + lax.rem(a + d, az_count // 2)
+            source_rows = pl.ds(
+                pl.multiple_of(b * local_rows - skipped, BAND_BINS), local_rows
+            )
+            target = turned_ref.at[a, :, whole_rows, cols]
+
+            @pl.when(b == a)
+            def _():
+                pltpu.make_async_copy(
+                    source.at[:, source_rows, here], target, out_recv.at[0]
+                ).start()
+
+            @pl.when(b != a)
+            def _():
+                pltpu.make_async_remote_copy(
+                    src_ref=source.at[:, source_rows, here],
+                    dst_ref=target,
+                    send_sem=out_send.at[c],
+                    recv_sem=out_recv.at[0],
+                    device_id=(b, g),
+                    device_id_type=MESH,
+                ).start()
+
+            return 0
+
+        lax.fori_loop(0, az_count // 2, one_block, 0)
+
     def chunk(c, _):
         cols = columns(c)
         own_load(c).wait()
@@ -262,24 +298,55 @@
         def _():
             rim_copy(c).wait_recv()
 
-        def block(i, _):
+        swapped = (c == 0) & (a <= middle)
+
+        def block(k, _):
+            i = lax.rem(k + jnp.where(swapped, half_blocks, 0), 2 * half_blocks)
             start = pl.multiple_of(i * block_rows, block_rows)
             total = mm(w_ref[0], window[0, pl.ds(start, span), cols], NN)
             total = total + mm(w_ref[1], window[1, pl.ds(start, span), cols], NN)
             total = total.astype(jnp.bfloat16)
-            window[0, pl.ds(start, block_rows), cols] = total[:block_rows]
-            window[1, pl.ds(start, block_rows), cols] = total[block_rows:]
-            return 0
-
-        lax.fori_loop(0, rows // block_rows, block, 0)
-
-        @pl.when(early)
-        def _():
-            send_blocks(0, local_rows, cols, c, 0)
-
-        @pl.when(has_before & early)
-        def _():
-            rim_sent(c)
+
+            @pl.when(swapped & (i >= half_blocks))
+            def _():
+                held = pl.ds(pl.multiple_of(start - half_rows, block_rows), block_rows)
+                ahead[0, held, :] = total[:block_rows]
+                ahead[1, held, :] = total[block_rows:]
+
+            @pl.when(jnp.logical_not(swapped & (i >= half_blocks)))
+            def _():
+                window[0, pl.ds(start, block_rows), cols] = total[:block_rows]
+                window[1, pl.ds(start, block_rows), cols] = total[block_rows:]
+
+            return 0
+
+        lax.fori_loop(0, half_blocks, block, 0)
+
+        @pl.when(early & jnp.logical_not(swapped))
+        def _():
+            send_half(window, 0, 0, cols, c)
+
+        @pl.when(early & swapped)
+        def _():
+            send_half(ahead, half_rows, az_count // 2, cols, c)
+
+        lax.fori_loop(half_blocks, 2 * half_blocks, block, 0)
+
+        @pl.when(swapped)
+        def _():
+            window[:, half_rows:rows, cols] = ahead[...]
+
+        @pl.when(early & jnp.logical_not(swapped))
+        def _():
+            send_half(window, 0, az_count // 2, cols, c)
+
+        @pl.when(early & swapped)
+        def _():
+            send_half(window, 0, 0, cols, c)
+
+        @pl.when(has_before & early & (c >= 2))
+        def _():
+            rim_sent(c - 2)
 
         return 0
 
@@ -303,6 +370,11 @@
 
     def send_phase(p):
         send_blocks(starts[p] * BAND_BINS, height_of(p), whole_lines, p, p)
+
+    @pl.when(has_before & early)
+    def _():
+        for c in range(max(0, chunks - 2), chunks):
+            rim_copy(c).wait_send()
 
     def height_of(p):
         return (starts[p + 1] - starts[p]) * BAND_BINS
@@ -544,6 +616,7 @@
         out_specs=[anywhere, anywhere],
         scratch_shapes=[
             pltpu.VMEM((2, rows + taps, lines), jnp.bfloat16),
+            pltpu.VMEM((2, rows // 2, width), jnp.bfloat16),
             pltpu.VMEM((2, 2 * block_rows, span), jnp.bfloat16),
             pltpu.VMEM((2, az_count, 2, BAND_BINS, lines), jnp.bfloat16),
             pltpu.VMEM((BAND_BINS, 2 * SIDE, SIDE), jnp.float32),

time: 447 us -> 443 us (level)
  Pallas kernels: 444 us -> 439 us
    pallas_call x1, Pallas kernels: 422 us -> 416 us  [exchange(): pl.pallas_call(functools.partial(exchange_kernel, width, block_rows), out...]
where the time goes in v6:
time: 443 us; the launch traced here: 439 us
  Pallas kernels  439 us (99%)
    pallas_call x1, Pallas kernels, exchange(): pl.pallas_call(functools.partial(exchange_kernel, width, block_rows), out...  416 us
    pallas_call x1, Pallas kernels, finish(): pl.pallas_call(finish_kernel, out_shape=jax.ShapeDtypeStruct((2, local_ro...  22.5 us

profile of v6, /device:TPU:29, one launch (start us, length us, event | category | flops | bytes accessed | tf_op | source)
XLA Modules:
  0.0 438.8 jit_solution(12607955257913261497)
XLA Ops:
  0.0 416.3 %exchange.1 = (bf16[8,2,288,2048]{3,2,1,0:T(8,128)(2,1)}, bf16[256,128,256]{2,1,0:T(8,128)(2,1)}) custom-call(s32[8,512]{1,0:T(8,128)} %bitcast.2, s32[512]{0:T(512)} %count_ref.1, f32[8,512]{1,0:T(8,128)} %bitcast.3, f32[512]{0:T(512)} %rate_ref.1, bf16[2,2048]{1,0:T(2,128)(2,1)} %replica_ref.1, bf16[2,256,256]{2,1,0:T(8,128)(2,1)} %constant.27.ftable_ref, ...), custom_call_target="tpu_custom_call" | custom-call | flops 146028888064 | bytes 83886080 | tf_op jit(solution)/shard_map/exchange/pallas_call | solution.py:609
  416.3 22.5 %finish.1 = f32[2,256,16384]{2,1,0:T(8,128)} custom-call(bf16[2,256,256]{2,1,0:T(8,128)(2,1)} %constant.22.itable_ref.table_ref, bf16[256,128,256]{2,1,0:T(8,128)(2,1)} %get-tuple-element.6.inner_ref), custom_call_target="tpu_custom_call" | custom-call | tf_op jit(solution)/shard_map/finish/pallas_call | solution.py:667
